TPU v7x, 32 devices: a whole 2x2x4 slice. The times are simulated.
32 devices in a mesh: dp: 16 (over z, y, core), tensor: 2 (over x).
Axes of the slice: x: 2, y: 2, z: 4, core: 2. Of those that a mesh axis runs over, the one named last changes fastest.
Arguments:
- tokens: bfloat16 [32768, 768], P(('dp', 'tensor')), may hold values from -6 to 6
- grad_values: bfloat16 [32768, 768], P(('dp', 'tensor')), may hold values from -6 to 6
- span_starts: int32 [64, 13], P('dp'), may hold values from 0 to 506
- w_qkv: bfloat16 [768, 3, 768], P(None, None, 'tensor'), may hold values from -0.21875 to 0.21875
- b_qv: float32 [2, 768], P(None, 'tensor'), may hold values from -3 to 3
- w_out: bfloat16 [768, 768], P('tensor'), may hold values from -0.875 to 0.875
- b_out: float32 [768], replicated, may hold values from -3 to 3
- ln1_gain: float32 [768], replicated, may hold values from 0.5 to 1.5
- ln1_bias: float32 [768], replicated, may hold values from -3 to 3
- w_in: bfloat16 [768, 3072], P(None, 'tensor'), may hold values from -0.21875 to 0.21875
- b_in: float32 [3072], P('tensor'), may hold values from -3 to 3
- w_down: bfloat16 [3072, 768], P('tensor'), may hold values from -0.109375 to 0.109375
- b_down: float32 [768], replicated, may hold values from -3 to 3
- ln2_gain: float32 [768], replicated, may hold values from 0.5 to 1.5
- ln2_bias: float32 [768], replicated, may hold values from -3 to 3
Outputs:
- mixed: bfloat16 [32768, 768], P(('dp', 'tensor'))
- d_tokens: float32 [32768, 768], P(('dp', 'tensor'))
- d_w_qkv: float32 [768, 3, 768], P(None, None, 'tensor')
- d_b_qv: float32 [2, 768], P(None, 'tensor')
- d_w_out: float32 [768, 768], P('tensor')
- d_b_out: float32 [768], replicated
- d_ln1_gain: float32 [768], replicated
- d_ln1_bias: float32 [768], replicated
- d_w_in: float32 [768, 3072], P(None, 'tensor')
- d_b_in: float32 [3072], P('tensor')
- d_w_down: float32 [3072, 768], P('tensor')
- d_b_down: float32 [768], replicated
- d_ln2_gain: float32 [768], replicated
- d_ln2_bias: float32 [768], replicated
Inputs may be any that keep to these rules, and one draw needn't show every extreme that they name: `span_starts`: a span covers 6 positions from its start, within its sequence; spans of one sequence may intersect.
All inputs are finite; a program needn't handle non-finite values.
Results may differ from a plain program's by a relative error of at most 0.013.
The roundings to bfloat16 on the way count: a program that leaves them out, or rounds other values in their place, can miss the bound.
Values may be sent and summed in bfloat16 or wider, within the bound.
No kernel may reach another device: no remote copies, remote signals or barrier semaphores. Data moves between devices by JAX's collectives and lax.ppermute only.
A program may use at most 192 MiB of HBM per device.

v0:
```python
import jax
import jax.numpy as jnp
from jax import lax
from jax.sharding import PartitionSpec as P

HEAD = 64
SPAN = 6


EPSILON = 1e-05


def layer_norm(values, gain_vec, bias_vec):
    average = jnp.mean(values, axis=-1, keepdims=True)
    centered = values - average
    variance = jnp.mean(centered * centered, axis=-1, keepdims=True)
    return centered * lax.rsqrt(variance + EPSILON) * gain_vec + bias_vec


def smooth_gate(values):
    return jax.nn.gelu(values, approximate=True)


def attend_forward(packed):
    queries = packed[:, 0]
    keys_seq = packed[:, 1]
    values_seq = packed[:, 2]
    scores = jnp.einsum(
        "qhe,khe->hqk", queries, keys_seq, preferred_element_type=jnp.float32
    ) * HEAD ** (-0.5)
    top_score = jnp.max(scores, axis=-1, keepdims=True)
    exponent = jnp.exp(scores - top_score)
    total = jnp.sum(exponent, axis=-1, keepdims=True)
    attn_weights = (exponent / total).astype(jnp.bfloat16)
    context = jnp.einsum(
        "hqk,khe->qhe", attn_weights, values_seq, preferred_element_type=jnp.float32
    )
    log_total = top_score[:, :, 0] + jnp.log(total[:, :, 0])
    return (context.reshape(context.shape[0], -1).astype(jnp.bfloat16), log_total)


def attend_backward(inputs):
    packed, grad_context, log_total = inputs
    queries = packed[:, 0]
    keys_seq = packed[:, 1]
    values_seq = packed[:, 2]
    grad_heads = grad_context.reshape(queries.shape)
    scores = jnp.einsum(
        "qhe,khe->hqk", queries, keys_seq, preferred_element_type=jnp.float32
    ) * HEAD ** (-0.5)
    probs_full = jnp.exp(scores - log_total[:, :, None])
    attn_weights = probs_full.astype(jnp.bfloat16)
    grad_values_seq = jnp.einsum(
        "hqk,qhe->khe", attn_weights, grad_heads, preferred_element_type=jnp.float32
    )
    grad_probs = jnp.einsum(
        "qhe,khe->hqk", grad_heads, values_seq, preferred_element_type=jnp.float32
    )
    row_total = jnp.sum(grad_probs * probs_full, axis=-1, keepdims=True)
    grad_scores = (probs_full * (grad_probs - row_total)).astype(jnp.bfloat16)
    grad_queries = jnp.einsum(
        "hqk,khe->qhe", grad_scores, keys_seq, preferred_element_type=jnp.float32
    ) * HEAD ** (-0.5)
    grad_keys = jnp.einsum(
        "hqk,qhe->khe", grad_scores, queries, preferred_element_type=jnp.float32
    ) * HEAD ** (-0.5)
    stacked = jnp.stack([grad_queries, grad_keys, grad_values_seq], axis=1)
    return stacked.astype(jnp.bfloat16)


def body(
    tokens,
    grad_values,
    span_starts,
    w_qkv,
    b_qv,
    w_out,
    b_out,
    ln1_gain,
    ln1_bias,
    w_in,
    b_in,
    w_down,
    b_down,
    ln2_gain,
    ln2_bias,
):
    own_rows = tokens.shape[0]
    model_width = tokens.shape[1]
    seq_count = span_starts.shape[0]
    inner = w_qkv.shape[2]
    heads_here = inner // HEAD
    tensor_size = lax.axis_size("tensor")
    length = own_rows * tensor_size // seq_count
    start_row = lax.axis_index("tensor") * own_rows
    full_tokens = lax.all_gather(tokens, "tensor", axis=0, tiled=True)
    all_rows = full_tokens.shape[0]
    w_qkv_flat = w_qkv.reshape(model_width, 3 * inner)
    qkv_bias = jnp.concatenate([b_qv[0], jnp.zeros_like(b_qv[0]), b_qv[1]])
    qkv = (jnp.dot(full_tokens, w_qkv_flat, preferred_element_type=jnp.float32) + qkv_bias).astype(
        jnp.bfloat16
    )
    qkv_seqs = qkv.reshape(seq_count, length, 3, heads_here, HEAD)
    context_seqs, log_totals = lax.map(attend_forward, qkv_seqs)
    context = context_seqs.reshape(all_rows, inner)
    rows_part = context
    branch = (
        lax.psum_scatter(
            jnp.dot(rows_part, w_out, preferred_element_type=jnp.float32),
            "tensor",
            scatter_dimension=0,
            tiled=True,
        )
        + b_out
    )
    first_sum = tokens.astype(jnp.float32) + branch
    normed = layer_norm(first_sum, ln1_gain, ln1_bias)
    normed_full = lax.all_gather(normed.astype(jnp.bfloat16), "tensor", axis=0, tiled=True)
    pre_act = jnp.dot(normed_full, w_in, preferred_element_type=jnp.float32) + b_in
    hidden = smooth_gate(pre_act).astype(jnp.bfloat16)
    rows_part = hidden
    ffn_out = (
        lax.psum_scatter(
            jnp.dot(rows_part, w_down, preferred_element_type=jnp.float32),
            "tensor",
            scatter_dimension=0,
            tiled=True,
        )
        + b_down
    )
    second_sum = normed + ffn_out
    mixed = layer_norm(second_sum, ln2_gain, ln2_bias).astype(jnp.bfloat16)
    positions = jnp.arange(length, dtype=jnp.int32)
    begins = span_starts[:, :, None]
    inside = (positions[None, None, :] >= begins) & (positions[None, None, :] < begins + SPAN)
    span_rows = jnp.any(inside, axis=1).reshape(seq_count * length).astype(jnp.float32)
    span_mask = lax.dynamic_slice_in_dim(span_rows, start_row, own_rows, 0)
    cotangent = grad_values.astype(jnp.float32) * span_mask[:, None]
    norm_two, pull_two = jax.vjp(layer_norm, second_sum, ln2_gain, ln2_bias)
    g_second, d_ln2_gain, d_ln2_bias = pull_two(cotangent)
    g_ffn = g_second.astype(jnp.bfloat16)
    d_b_down = jnp.sum(g_ffn.astype(jnp.float32), axis=0)
    gate_value, gate_pull = jax.vjp(smooth_gate, pre_act)
    g_ffn_full = lax.all_gather(g_ffn, "tensor", axis=0, tiled=True)
    d_w_down = jnp.einsum("rf,rd->fd", hidden, g_ffn_full, preferred_element_type=jnp.float32)
    g_hidden = jnp.einsum("rd,fd->rf", g_ffn_full, w_down, preferred_element_type=jnp.float32)
    g_pre = gate_pull(g_hidden)[0].astype(jnp.bfloat16)
    d_w_in = jnp.einsum("rd,rf->df", normed_full, g_pre, preferred_element_type=jnp.float32)
    d_b_in = jnp.sum(g_pre.astype(jnp.float32), axis=0)
    rows_part = g_pre
    g_normed = g_second + lax.psum_scatter(
        jnp.einsum("rf,df->rd", rows_part, w_in, preferred_element_type=jnp.float32),
        "tensor",
        scatter_dimension=0,
        tiled=True,
    )
    norm_one, pull_one = jax.vjp(layer_norm, first_sum, ln1_gain, ln1_bias)
    g_first, d_ln1_gain, d_ln1_bias = pull_one(g_normed)
    g_branch = g_first.astype(jnp.bfloat16)
    d_b_out = jnp.sum(g_branch.astype(jnp.float32), axis=0)
    g_branch_full = lax.all_gather(g_branch, "tensor", axis=0, tiled=True)
    d_w_out = jnp.einsum("rc,rd->cd", context, g_branch_full, preferred_element_type=jnp.float32)
    g_context = jnp.einsum(
        "rd,cd->rc", g_branch_full, w_out, preferred_element_type=jnp.float32
    ).astype(jnp.bfloat16)
    g_context_seqs = g_context.reshape(seq_count, length, inner)
    g_qkv = lax.map(attend_backward, (qkv_seqs, g_context_seqs, log_totals)).reshape(
        all_rows, 3 * inner
    )
    d_w_qkv = jnp.einsum(
        "rd,rc->dc", full_tokens, g_qkv, preferred_element_type=jnp.float32
    ).reshape(model_width, 3, inner)
    column_sums = jnp.sum(g_qkv.astype(jnp.float32), axis=0).reshape(3, inner)
    d_b_qv = jnp.stack([column_sums[0], column_sums[2]])
    rows_part = g_qkv
    d_tokens = g_first + lax.psum_scatter(
        jnp.einsum("rc,dc->rd", rows_part, w_qkv_flat, preferred_element_type=jnp.float32).astype(
            jnp.bfloat16
        ),
        "tensor",
        scatter_dimension=0,
        tiled=True,
    ).astype(jnp.float32)
    d_b_out, d_ln1_gain, d_ln1_bias, d_b_down, d_ln2_gain, d_ln2_bias = lax.psum(
        (d_b_out, d_ln1_gain, d_ln1_bias, d_b_down, d_ln2_gain, d_ln2_bias), "tensor"
    )
    (
        d_w_qkv,
        d_b_qv,
        d_w_out,
        d_b_out,
        d_ln1_gain,
        d_ln1_bias,
        d_w_in,
        d_b_in,
        d_w_down,
        d_b_down,
        d_ln2_gain,
        d_ln2_bias,
    ) = lax.psum(
        (
            d_w_qkv,
            d_b_qv,
            d_w_out,
            d_b_out,
            d_ln1_gain,
            d_ln1_bias,
            d_w_in,
            d_b_in,
            d_w_down,
            d_b_down,
            d_ln2_gain,
            d_ln2_bias,
        ),
        "dp",
    )
    return (
        mixed,
        d_tokens,
        d_w_qkv,
        d_b_qv,
        d_w_out,
        d_b_out,
        d_ln1_gain,
        d_ln1_bias,
        d_w_in,
        d_b_in,
        d_w_down,
        d_b_down,
        d_ln2_gain,
        d_ln2_bias,
    )


def solution(mesh):
    placed = (
        P(("dp", "tensor"), None),
        P(("dp", "tensor"), None),
        P("dp", None),
        P(None, None, "tensor"),
        P(None, "tensor"),
        P("tensor", None),
        P(),
        P(),
        P(),
        P(None, "tensor"),
        P("tensor"),
        P("tensor", None),
        P(),
        P(),
        P(),
    )
    return jax.shard_map(
        body,
        mesh=mesh,
        in_specs=placed,
        out_specs=(
            P(("dp", "tensor"), None),
            P(("dp", "tensor"), None),
            P(None, None, "tensor"),
            P(None, "tensor"),
            P("tensor", None),
            P(),
            P(),
            P(),
            P(None, "tensor"),
            P("tensor"),
            P("tensor", None),
            P(),
            P(),
            P(),
        ),
        check_vma=False,
    )
```

profile of v0, /device:TPU:0, one launch (start us, length us, event | category | flops | bytes accessed | tf_op | source)
XLA Modules:
  0.0 956.2 jit_solution(17968625957682814721)
XLA Ops:
  8.0 3.9 copy.53
  11.9 45.3 %all-gather.5.cloned.1.call-done = bf16[2048,768]{1,0:T(8,128)(2,1)} async-done(((bf16[1024,768]{1,0:T(8,128)(2,1)}), bf16[2048,768]{1,0:T(8,128)(2,1)}) %all-gather.5.cloned.1.call-update) | async-done | bytes 3145744 | tf_op jit(solution)/shard_map/all_gather | solution.py:96
  57.2 8.9 add_convert_fusion
  66.2 6.6 copy.54
  72.8 8.8 reshape.215
  81.6 5.6 copy.55
  87.3 23.6 %while.22 = (s32[]{:T(128)}, bf16[4,512,384]{2,1,0:T(8,128)(2,1)}, f32[4,6,512]{2,1,0:T(8,128)S(1)}, bf16[4,512,3,6,64]{1,4,3,2,0:T(8,128)(2,1)}, s32[]{:T(128)}) while((s32[]{:T(128)}, bf16[4,512,384]{2,1,0:T(8,128)(2,1)}, f32[4,6,512]{2,1,0:T(8,128)S(1)}, bf16[4,512,3,6,64]{1,4,3,2,0:T(8,128)(2,1)}, s32[]{:T(128)}) %tuple.63), condition=%wide.region_3.4_spmd, body=%wide.region_0.3_spmd.sunk | while | flops 417002496 | bytes 24498256 | solution.py:104
  90.7 1.4 fusion.89
  96.6 1.4 fusion.89
  102.5 1.4 fusion.89
  108.4 1.4 fusion.89
  110.8 6.0 fusion.42
  117.1 76.9 %reduce-scatter.5.cloned.1.call-done = f32[1024,768]{1,0:T(8,128)} async-done(((f32[2048,768]{1,0:T(8,128)}), f32[1024,768]{1,0:T(8,128)}) %reduce-scatter.5.cloned.1.call-update) | async-done | bytes 3145744 | tf_op jit(solution)/shard_map/reduce_scatter | solution.py:108
  194.0 2.8 fusion.40
  198.6 1.7 fusion.32
  200.3 45.1 %all-gather.7.cloned.1.call-done = bf16[2048,768]{1,0:T(8,128)(2,1)} async-done(((bf16[1024,768]{1,0:T(8,128)(2,1)}), bf16[2048,768]{1,0:T(8,128)(2,1)}) %all-gather.7.cloned.1.call-update) | async-done | bytes 3145744 | tf_op jit(solution)/shard_map/all_gather | solution.py:118
  245.4 12.7 %multiply_convert_fusion.1 = (bf16[2048,1536]{1,0:T(8,128)(2,1)S(1)}, f32[2048,1536]{1,0:T(8,128)}) fusion(f32[1536]{0:T(1024)S(1)} %copy-done.25, bf16[2048,768]{1,0:T(8,128)(2,1)} %all-gather.7.cloned.1.call-done, bf16[768,1536]{1,0:T(8,128)(2,1)S(1)} %copy-done), kind=kOutput, calls=%fused_computation.49 | convolution fusion | flops 4863295488 | bytes 24385536 | tf_op jit(solution)/shard_map/dot_general | solution.py:119
  258.0 2.6 copy-done.26
  260.7 6.9 fusion.43
  268.5 76.2 %reduce-scatter.7.cloned.1.call-done = f32[1024,768]{1,0:T(8,128)} async-done(((f32[2048,768]{1,0:T(8,128)}), f32[1024,768]{1,0:T(8,128)}) %reduce-scatter.7.cloned.1.call-update) | async-done | bytes 3145744 | tf_op jit(solution)/shard_map/reduce_scatter | solution.py:123
  344.7 3.9 fusion.39
  350.0 2.3 multiply_reduce_fusion.2
  352.3 2.8 fusion.38
  355.1 1.7 copy-done.4
  356.8 2.1 convert_reduce_fusion.2
  359.3 44.6 %all-gather.9.cloned.1.call-done = bf16[2048,768]{1,0:T(8,128)(2,1)} async-done(((bf16[1024,768]{1,0:T(8,128)(2,1)}), bf16[2048,768]{1,0:T(8,128)(2,1)}) %all-gather.9.cloned.1.call-update) | async-done | bytes 3145744 | tf_op jit(solution)/shard_map/all_gather | solution.py:144
  403.9 16.7 %convert_reduce_fusion = (f32[1536]{0:T(1024)S(1)}, bf16[2048,1536]{1,0:T(8,128)(2,1)S(1)}) fusion(f32[2048,1536]{1,0:T(8,128)} %get-tuple-element.159, f32[1536]{0:T(1024)S(1)} %copy-done.25, bf16[2048,768]{1,0:T(8,128)(2,1)} %all-gather.9.cloned.1.call-done, bf16[1536,768]{1,0:T(8,128)(2,1)} %param.30), kind=kOutput, calls=%fused_computation.48 | convolution fusion | flops 4904188416 | bytes 24391680 | tf_op jit(solution)/shard_map/rd,fd->rf/dot_general | solution.py:146
  420.7 2.6 copy-done.27
  423.3 6.9 fusion.44
  430.3 77.2 %reduce-scatter.9.cloned.1.call-done = f32[1024,768]{1,0:T(8,128)} async-done(((f32[2048,768]{1,0:T(8,128)}), f32[1024,768]{1,0:T(8,128)}) %reduce-scatter.9.cloned.1.call-update) | async-done | bytes 3145744 | tf_op jit(solution)/shard_map/reduce_scatter | solution.py:151
  507.4 4.6 multiply_reduce_fusion.3
  512.1 2.8 fusion.37
  514.9 1.6 copy-done.3
  516.6 1.5 convert_reduce_fusion.3
  518.3 44.9 %all-gather.11.cloned.1.call-done = bf16[2048,768]{1,0:T(8,128)(2,1)} async-done(((bf16[1024,768]{1,0:T(8,128)(2,1)}), bf16[2048,768]{1,0:T(8,128)(2,1)}) %all-gather.11.cloned.1.call-update) | async-done | bytes 3145744 | tf_op jit(solution)/shard_map/all_gather | solution.py:161
  563.1 4.9 convolution_convert_fusion.1
  568.0 45.1 %while.23 = (s32[]{:T(128)}, bf16[4,512,3,6,64]{1,4,3,2,0:T(8,128)(2,1)}, bf16[4,512,3,6,64]{1,4,3,2,0:T(8,128)(2,1)}, f32[4,6,512]{2,1,0:T(8,128)S(1)}, bf16[4,512,384]{2,1,0:T(8,128)(2,1)}, /*index=5*/s32[]{:T(128)}) while((s32[]{:T(128)}, bf16[4,512,3,6,64]{1,4,3,2,0:T(8,128)(2,1)}, bf16[4,512,3,6,64]{1,4,3,2,0:T(8,128)(2,1)}, ...), condition=%wide.region_18.19_spmd, body=%wide.region_16.18_spmd.sunk | while | flops 1030026240 | bytes 57499740 | solution.py:167
  569.2 1.4 dynamic-slice_bitcast_fusion.7
  572.8 1.7 multiply_reduce_fusion.11
  574.5 1.9 multiply_convert_fusion.3
  580.5 1.4 dynamic-slice_bitcast_fusion.7
  584.1 1.7 multiply_reduce_fusion.11
  585.7 1.9 multiply_convert_fusion.3
  595.3 1.7 multiply_reduce_fusion.11
  597.0 1.9 multiply_convert_fusion.3
  606.5 1.7 multiply_reduce_fusion.11
  608.2 1.9 multiply_convert_fusion.3
  613.1 6.4 copy.61
  619.5 2.0 copy.71
  621.5 2.2 copy-done.6
  623.7 5.8 convolution_convert_fusion
  629.6 10.1 %fusion.48 = f32[1536,768]{1,0:T(8,128)} fusion(bf16[2048,1536]{1,0:T(8,128)(2,1)} %copy-done.26, bf16[2048,768]{1,0:T(8,128)(2,1)} %all-gather.9.cloned.1.call-done), kind=kOutput, calls=%fused_computation.107 | convolution fusion | flops 4831838208 | bytes 14155776 | tf_op jit(solution)/shard_map/rf,rd->fd/dot_general | solution.py:145
  639.7 9.6 %fusion.47 = f32[768,1536]{1,0:T(8,128)} fusion(bf16[2048,768]{1,0:T(8,128)(2,1)S(1)} %copy-done.23, bf16[2048,1536]{1,0:T(8,128)(2,1)} %copy-done.27), kind=kOutput, calls=%fused_computation.106 | convolution fusion | flops 4831838208 | bytes 14155776 | tf_op jit(solution)/shard_map/rd,rf->df/dot_general | solution.py:148
  649.4 5.7 fusion.45
  655.0 5.3 copy.62
  660.3 4.3 fusion.46
  665.4 7.4 all-reduce.2
  672.7 3.1 convert_reduce_fusion.1
  676.0 64.1 %all-reduce = (f32[2,384]{1,0:T(2,128)}, f32[768]{0:T(1024)}, f32[768]{0:T(1024)}, f32[768]{0:T(1024)}, f32[1536]{0:T(1024)}, /*index=5*/f32[768]{0:T(1024)}, f32[768]{0:T(1024)}, f32[768]{0:T(1024)}) all-reduce(f32[2,384]{1,0:T(2,128)S(1)} %pad_maximum_fusion.1, ...), channel_id=1, replica_groups=mesh['dp'=16,'tensor'=2] {'dp'}, use_global_device_ids=true, to_apply=%region_22.23 | all-reduce | flops 6912 | bytes 55296 | tf_op jit(solution)/shard_map/psum | solution.py:200
  740.1 4.5 convert_add_fusion
  744.6 193.9 %all-reduce.5.cloned.1.call-done = (f32[768,3,384]{2,0,1:T(8,128)}, f32[384,768]{1,0:T(8,128)}, f32[768,1536]{1,0:T(8,128)}, f32[1536,768]{1,0:T(8,128)}) async-done(((f32[768,3,384]{2,0,1:T(8,128)}, f32[384,768]{1,0:T(8,128)}, f32[768,1536]{1,0:T(8,128)}, f32[1536,768]{1,0:T(8,128)}), (f32[768,3,384]{2,0,1:T(8,128)}, f32[384,768]{1,0:T(8,128)}, f32[768,1536]{1,0:T(8,128)}, ...) | async-done | bytes 14155792 | tf_op jit(solution)/shard_map/psum | solution.py:200
  938.4 4.2 copy.100
  943.7 2.4 copy.102
  947.1 2.2 copy.103
  (171 shorter events, 54.5 us)
Async XLA Ops:
  7.2 238.2 %copy-start = (bf16[768,1536]{1,0:T(8,128)(2,1)S(1)}, bf16[768,1536]{1,0:T(8,128)(2,1)}, u32[]{:S(2)}) copy-start(bf16[768,1536]{1,0:T(8,128)(2,1)} %param.28) | copy-start | bytes 7077892
  7.2 4.7 copy-start.21
  7.2 50.0 %all-gather.5.cloned.1.call-start = ((), (), s32[]{:S(2)}) async-start(), calls=%async_computation.4 | async-start | bytes 4718592 | tf_op jit(solution)/shard_map/all_gather | solution.py:96
  7.9 186.1 %reduce-scatter.5.cloned.1.call-start = ((), (), s32[]{:S(2)}) async-start(), calls=%async_computation.5 | async-start | bytes 9437184 | tf_op jit(solution)/shard_map/reduce_scatter | solution.py:108
  116.8 77.2 %copy-start.19 = (f32[768]{0:T(1024)S(1)}, f32[768]{0:T(1024)}, u32[]{:S(2)}) copy-start(f32[768]{0:T(1024)} %param.25) | copy-start | bytes 9220
  116.8 128.5 %all-gather.7.cloned.1.call-start = ((), (), s32[]{:S(2)}) async-start(), calls=%async_computation.6 | async-start | bytes 4718592 | tf_op jit(solution)/shard_map/all_gather | solution.py:118
  196.9 1.7 copy-start.2
  196.9 1.7 copy-start.11
  196.9 1.6 copy-start.13
  198.6 46.8 %copy-start.25 = (f32[1536]{0:T(1024)S(1)}, f32[1536]{0:T(1024)}, u32[]{:S(2)}) copy-start(f32[1536]{0:T(1024)} %param.29) | copy-start | bytes 18436
  200.3 144.5 %reduce-scatter.7.cloned.1.call-start = ((), (), s32[]{:S(2)}) async-start(), calls=%async_computation.7 | async-start | bytes 9437184 | tf_op jit(solution)/shard_map/reduce_scatter | solution.py:123
  245.4 15.3 %copy-start.24 = (bf16[1536,768]{1,0:T(8,128)(2,1)S(1)}, bf16[1536,768]{1,0:T(8,128)(2,1)}, u32[]{:S(2)}) copy-start(bf16[1536,768]{1,0:T(8,128)(2,1)} %param.30) | copy-start | bytes 7077892
  258.0 2.6 copy-start.26
  267.5 0.7 copy-start.17
  267.5 77.2 %copy-start.20 = (f32[768]{0:T(1024)S(1)}, f32[768]{0:T(1024)}, u32[]{:S(2)}) copy-start(f32[768]{0:T(1024)} %param.31) | copy-start | bytes 9220
  267.5 136.4 %all-gather.9.cloned.1.call-start = ((), (), s32[]{:S(2)}) async-start(), calls=%async_computation.8 | async-start | bytes 4718592 | tf_op jit(solution)/shard_map/all_gather | solution.py:144
  348.6 1.4 copy-start.5
  348.6 1.4 copy-start.12
  349.2 3.1 copy-start.18
  355.1 1.7 copy-start.4
  358.9 148.6 %reduce-scatter.9.cloned.1.call-start = ((), (), s32[]{:S(2)}) async-start(), calls=%async_computation.9 | async-start | bytes 9437184 | tf_op jit(solution)/shard_map/reduce_scatter | solution.py:151
  420.6 2.7 copy-start.27
  430.2 132.9 %all-gather.11.cloned.1.call-start = ((), (), s32[]{:S(2)}) async-start(), calls=%async_computation.10 | async-start | bytes 4718592 | tf_op jit(solution)/shard_map/all_gather | solution.py:161
  514.9 1.6 copy-start.3
  516.6 46.6 %copy-start.10 = (bf16[384,768]{1,0:T(8,128)(2,1)S(1)}, bf16[384,768]{1,0:T(8,128)(2,1)}, u32[]{:S(2)}) copy-start(bf16[384,768]{1,0:T(8,128)(2,1)} %param.24) | copy-start | bytes 1769476
  518.1 222.1 %reduce-scatter.11.cloned.1.call-start = ((), (), s32[]{:S(2)}) async-start(), calls=%async_computation.11 | async-start | bytes 4718592 | tf_op jit(solution)/shard_map/reduce_scatter | solution.py:176
  619.5 4.2 copy-start.8
  621.5 2.2 copy-start.6
  629.5 308.9 %all-reduce.5.cloned.1.call-start = ((), (), s32[]{:S(2)}) async-start(), calls=%async_computation.12 | async-start | bytes 28311552 | tf_op jit(solution)/shard_map/psum | solution.py:200
  629.6 10.1 %copy-start.23 = (bf16[2048,768]{1,0:T(8,128)(2,1)S(1)}, bf16[2048,768]{1,0:T(8,128)(2,1)}, u32[]{:S(2)}) copy-start(bf16[2048,768]{1,0:T(8,128)(2,1)} %all-gather.7.cloned.1.call-done) | copy-start | bytes 9437188
  629.6 19.7 %slice-start.4 = ((s8[4718592]{0:T(1024)(128)(4,1)}), s8[4194304]{0:T(1024)(128)(4,1)S(1)}, s32[]{:S(2)}) async-start(s8[4718592]{0:T(1024)(128)(4,1)} %bitcast.145), calls=%async_computation.17 | async-start | bytes 8388608
  639.7 9.7 %slice-start.5 = ((s8[4718592]{0:T(1024)(128)(4,1)}), s8[524288]{0:T(1024)(128)(4,1)S(1)}, s32[]{:S(2)}) async-start(s8[4718592]{0:T(1024)(128)(4,1)} %bitcast.145), calls=%async_computation.18 | async-start | bytes 1048576
  639.7 9.7 %copy-start.22 = (bf16[2048,768]{1,0:T(8,128)(2,1)S(1)}, bf16[2048,768]{1,0:T(8,128)(2,1)}, u32[]{:S(2)}) copy-start(bf16[2048,768]{1,0:T(8,128)(2,1)} %all-gather.5.cloned.1.call-done) | copy-start | bytes 9437188
  655.0 5.3 copy-start.7
  664.7 0.7 copy-start.14
  664.7 0.7 copy-start.15
  664.7 0.7 copy-start.16
  938.4 5.2 slice-start.2
  938.4 4.2 copy-start.9
  938.4 5.2 slice-start.3
  942.6 4.1 slice-start
  943.6 3.4 slice-start.1
  943.6 5.6 copy-start.1
Sparse Core Ops, SparseCore 0:
  9.6 47.6 all-gather.4
  117.0 77.0 reduce-scatter.4
  200.4 44.9 all-gather.6
  267.7 77.0 reduce-scatter.6
  359.0 44.9 all-gather.8
  430.4 77.0 reduce-scatter.8
  518.2 44.9 all-gather.10
  629.7 43.7 reduce-scatter.10
  679.1 259.2 all-reduce.4
where the time goes:
time: 966 us; the launch traced here: 956 us
  waiting for transfers between devices  605 us (63%)
  matrix products  130 us (13%)
  local copies, waits for them, and re-layouts  83.8 us (9%)
  blocking collectives  71.4 us (7%)
  other arithmetic  49.4 us (5%)
  between operations  14.7 us (2%)
    psum x1, waiting for transfers between devices, body(): lax.psum((d_w_qkv, d_b_qv, d_w_out, d_b_out, d_ln1_gain, d_ln1_bias, d_w_...  194 us
    reduce_scatter x1, waiting for transfers between devices, body(): lax.psum_scatter(jnp.einsum('rf,df->rd', rows_part, w_in, preferred_eleme...  77.2 us
    reduce_scatter x1, waiting for transfers between devices, body(): lax.psum_scatter(jnp.dot(rows_part, w_out, preferred_element_type=jnp.flo...  76.9 us
    reduce_scatter x1, waiting for transfers between devices, body(): lax.psum_scatter(jnp.dot(rows_part, w_down, preferred_element_type=jnp.fl...  76.2 us
    psum x1, blocking collectives, body(): lax.psum((d_w_qkv, d_b_qv, d_w_out, d_b_out, d_ln1_gain, d_ln1_bias, d_w_...  64.1 us
    all_gather x1, waiting for transfers between devices, body(): full_tokens = lax.all_gather(tokens, 'tensor', axis=0, tiled=True)  45.3 us
    all_gather x1, waiting for transfers between devices, body(): lax.all_gather(normed.astype(jnp.bfloat16), 'tensor', axis=0, tiled=True)  45.1 us
    all_gather x1, waiting for transfers between devices, body(): g_branch_full = lax.all_gather(g_branch, 'tensor', axis=0, tiled=True)  44.9 us
  transfers between devices with their start and end apart: 9, of which 8 were waited for; matrix products, arithmetic and copies ran while one was open for 5% of the time, Pallas kernels for 0%

commit v1 on v0

v1 whole, which is shorter than its diff:
```python
import jax
import jax.numpy as jnp
from jax import lax
from jax.experimental import pallas as pl
from jax.experimental.pallas import tpu as pltpu
from jax.sharding import PartitionSpec as P

HEAD = 64
SPAN = 6
LANES = 128
EPSILON = 1e-05
F32 = jnp.float32
BF16 = jnp.bfloat16
VMEM_LIMIT = 48 * 1024 * 1024


def flip(values, bit):
    size = lax.axis_size("dp")
    return lax.ppermute(values, "dp", [(at, at ^ (1 << bit)) for at in range(size)])


def flip_tensor(values):
    return lax.ppermute(values, "tensor", [(0, 1), (1, 0)])


def my_bit(bit):
    return (lax.axis_index("dp") >> bit) & 1


def in_order(mine, theirs, bit, axis=0):
    upper = my_bit(bit) == 1
    first = jnp.where(upper, theirs, mine)
    second = jnp.where(upper, mine, theirs)
    return jnp.concatenate([first, second], axis=axis)


def gather_other(shard, bits):
    rows = shard.shape[0]
    pieces = 1 << len(bits)
    place = sum(my_bit(bit) << (len(bits) - 1 - at) for at, bit in enumerate(bits))
    piece = lax.dynamic_slice_in_dim(shard, place * (rows // pieces), rows // pieces, 0)
    held = flip_tensor(piece)
    for bit in reversed(bits):
        held = in_order(held, flip(held, bit), bit)
    return held


def split_by(values, bit):
    halves = values.reshape((2, values.shape[0] // 2) + values.shape[1:])
    at = my_bit(bit)
    keep = lax.dynamic_index_in_dim(halves, at, 0, keepdims=False)
    send = lax.dynamic_index_in_dim(halves, 1 - at, 0, keepdims=False)
    return keep, send


def scatter_sum(values, bit):
    keep, send = split_by(values, bit)
    return keep + flip(send.astype(BF16), bit).astype(F32)


def spread(values, bits):
    held = lax.optimization_barrier(values.astype(BF16))
    for bit in bits:
        held = in_order(held, flip(held, bit), bit)
    return held


def lane_halves(rows):
    return lax.broadcasted_iota(jnp.int32, (rows, LANES), 1) < HEAD


def dot_nt(left, right):
    return lax.dot_general(left, right, (((1,), (1,)), ((), ())), preferred_element_type=F32)


def dot_tn(left, right):
    return lax.dot_general(left, right, (((0,), (0,)), ((), ())), preferred_element_type=F32)


def two_heads(block):
    low = lane_halves(block.shape[0])
    zero = jnp.zeros_like(block)
    return jnp.concatenate([jnp.where(low, block, zero), jnp.where(low, zero, block)], axis=0)


def softmax_rows(scores):
    exponent = jnp.exp(scores - jnp.max(scores, axis=-1, keepdims=True))
    return exponent * (1.0 / jnp.sum(exponent, axis=-1, keepdims=True))


def attend_kernel(q_ref, k_ref, v_ref, out_ref):
    rows = q_ref.shape[0]
    low = lane_halves(rows)
    both = two_heads(q_ref[...])
    probs = softmax_rows(dot_nt(both, k_ref[...]) * HEAD ** (-0.5)).astype(BF16)
    mixed = jnp.dot(probs, v_ref[...], preferred_element_type=F32)
    out_ref[...] = jnp.where(low, mixed[:rows], mixed[rows:]).astype(BF16)


def attend(queries, keys, values, seqs):
    q_rows, length, inner = queries.shape[0] // seqs, keys.shape[0] // seqs, keys.shape[1]
    tile = min(q_rows, 256)
    tiles = q_rows // tile
    q_spec = pl.BlockSpec((tile, LANES), lambda s, j, i: (s * tiles + i, j))
    kv_spec = pl.BlockSpec((length, LANES), lambda s, j, i: (s, j))
    return pl.pallas_call(
        attend_kernel,
        grid=(seqs, inner // LANES, tiles),
        in_specs=[q_spec, kv_spec, kv_spec],
        out_specs=q_spec,
        out_shape=jax.ShapeDtypeStruct(queries.shape, BF16),
        compiler_params=pltpu.CompilerParams(vmem_limit_bytes=VMEM_LIMIT),
        cost_estimate=pl.CostEstimate(
            flops=16 * q_rows * length * inner * seqs,
            bytes_accessed=2 * (2 * queries.size + 2 * keys.size),
            transcendentals=seqs * q_rows * length * inner // HEAD,
        ),
    )(queries, keys, values)


def attend_back_kernel(q_ref, k_ref, v_ref, g_ref, dq_ref, dk_ref, dv_ref):
    rows = q_ref.shape[0]
    low = lane_halves(rows)
    both, grads = two_heads(q_ref[...]), two_heads(g_ref[...])
    probs = softmax_rows(dot_nt(both, k_ref[...]) * HEAD ** (-0.5))
    grad_probs = dot_nt(grads, v_ref[...])
    dv_ref[...] = dot_tn(probs.astype(BF16), grads).astype(BF16)
    row_total = jnp.sum(grad_probs * probs, axis=-1, keepdims=True)
    grad_scores = (probs * (grad_probs - row_total)).astype(BF16)
    dq = jnp.dot(grad_scores, k_ref[...], preferred_element_type=F32) * HEAD ** (-0.5)
    dq_ref[...] = jnp.where(low, dq[:rows], dq[rows:]).astype(BF16)
    dk_ref[...] = (dot_tn(grad_scores, both) * HEAD ** (-0.5)).astype(BF16)


def attend_back(queries, keys, values, grads, seqs):
    q_rows, length, inner = queries.shape[0] // seqs, keys.shape[0] // seqs, keys.shape[1]
    q_spec = pl.BlockSpec((q_rows, LANES), lambda s, j: (s, j))
    kv_spec = pl.BlockSpec((length, LANES), lambda s, j: (s, j))
    return pl.pallas_call(
        attend_back_kernel,
        grid=(seqs, inner // LANES),
        in_specs=[q_spec, kv_spec, kv_spec, q_spec],
        out_specs=[q_spec, kv_spec, kv_spec],
        out_shape=[
            jax.ShapeDtypeStruct(queries.shape, BF16),
            jax.ShapeDtypeStruct(keys.shape, BF16),
            jax.ShapeDtypeStruct(keys.shape, BF16),
        ],
        compiler_params=pltpu.CompilerParams(vmem_limit_bytes=VMEM_LIMIT),
        cost_estimate=pl.CostEstimate(
            flops=40 * q_rows * length * inner * seqs,
            bytes_accessed=2 * (3 * queries.size + 4 * keys.size),
            transcendentals=seqs * q_rows * length * inner // HEAD,
        ),
    )(queries, keys, values, grads)


def norm_rows(values):
    average = jnp.mean(values, axis=-1, keepdims=True)
    centered = values - average
    variance = jnp.mean(centered * centered, axis=-1, keepdims=True)
    root = lax.rsqrt(variance + EPSILON)
    return centered * root, root


def norm_back(grad, unit, root, gain):
    grad_y = grad * gain
    inner = jnp.mean(grad_y, axis=-1, keepdims=True)
    along = jnp.mean(grad_y * unit, axis=-1, keepdims=True)
    return root * (grad_y - inner - unit * along)


def gelu(values):
    return jax.nn.gelu(values, approximate=True)


def gelu_and_slope(values):
    gate, pull = jax.vjp(gelu, values)
    return gate, pull(jnp.ones_like(values))[0]


def mm(left, right):
    return jnp.dot(left, right, preferred_element_type=F32)


def body(
    tokens,
    grad_values,
    span_starts,
    w_qkv,
    b_qv,
    w_out,
    b_out,
    ln1_gain,
    ln1_bias,
    w_in,
    b_in,
    w_down,
    b_down,
    ln2_gain,
    ln2_bias,
):
    rows, width = tokens.shape
    inner = w_qkv.shape[2]
    hidden_half = w_in.shape[1]
    halves = lax.axis_size("tensor")
    seqs = span_starts.shape[0] // halves
    spans = span_starts.shape[1]
    length = rows // seqs
    half_at = lax.axis_index("tensor")
    dp_size = lax.axis_size("dp")
    bits = dp_size.bit_length() - 1

    w_qkv_own = jnp.transpose(w_qkv, (1, 0, 2)).reshape(3 * width, inner)
    bias_pack = jnp.concatenate([b_qv[0], b_qv[1], b_in]).reshape(-1, LANES)
    bias_other = flip_tensor(bias_pack).reshape(-1)
    w_qkv_oth = gather_other(w_qkv_own, (0, 2, 1))
    w_out_oth = gather_other(w_out, (0, 1, 2))
    w_in_oth = gather_other(w_in, (0, 2, 1))
    w_down_oth = gather_other(w_down, (0, 1, 2))
    w_qkv_both = [w_qkv_own.reshape(3, width, inner), w_qkv_oth.reshape(3, width, inner)]
    w_out_both = [w_out, w_out_oth]
    w_in_both = [w_in, w_in_oth]
    w_down_both = [w_down, w_down_oth]
    b_q_both = [b_qv[0], bias_other[:inner]]
    b_v_both = [b_qv[1], bias_other[inner : 2 * inner]]
    b_in_both = [b_in, bias_other[2 * inner :]]

    starts = lax.dynamic_slice_in_dim(span_starts, half_at * seqs, seqs, 0)
    places = starts[:, :, None] + jnp.arange(SPAN, dtype=jnp.int32)
    earlier = jnp.tril(jnp.ones((spans, spans), jnp.bool_), -1)
    covered = (places[:, :, :, None] >= starts[:, None, None, :]) & (
        places[:, :, :, None] < starts[:, None, None, :] + SPAN
    )
    fresh = ~jnp.any(covered & earlier[None, :, None, :], axis=-1)
    slots = -(-spans * SPAN // 16) * 16
    pad = slots - spans * SPAN
    places = jnp.pad(places.reshape(seqs, spans * SPAN), ((0, 0), (0, pad)))
    fresh = jnp.pad(fresh.reshape(seqs, spans * SPAN), ((0, 0), (0, pad)))
    picks = (places[:, :, None] == jnp.arange(length, dtype=jnp.int32)).astype(BF16)
    few = seqs * slots

    def pick(values):
        return jnp.einsum(
            "srt,std->srd", picks, values.reshape(seqs, length, width), preferred_element_type=F32
        ).reshape(few, width)

    tokens_few = pick(tokens).astype(BF16)
    grad_few = pick(grad_values) * fresh.reshape(few, 1).astype(F32)

    keys, values, queries_few, context_few = [], [], [], []
    for at in range(2):
        w_q, w_k, w_v = w_qkv_both[at][0], w_qkv_both[at][1], w_qkv_both[at][2]
        keys.append(mm(tokens, w_k).astype(BF16))
        values.append((mm(tokens, w_v) + b_v_both[at]).astype(BF16))
        queries_few.append((mm(tokens_few, w_q) + b_q_both[at]).astype(BF16))
        context_few.append(attend(queries_few[at], keys[at], values[at], seqs))
    branch_few = mm(context_few[0], w_out_both[0]) + mm(context_few[1], w_out_both[1]) + b_out
    unit_one, root_one = norm_rows(tokens_few.astype(F32) + branch_few)
    normed_few = unit_one * ln1_gain + ln1_bias
    normed_low = normed_few.astype(BF16)
    pre_few = [mm(normed_low, w_in_both[at]) + b_in_both[at] for at in range(2)]
    gates = [gelu_and_slope(pre) for pre in pre_few]
    ffn_few = mm(gates[0][0].astype(BF16), w_down) + mm(gates[1][0].astype(BF16), w_down_oth) + b_down
    unit_two, root_two = norm_rows(normed_few + ffn_few)

    g_second = norm_back(grad_few, unit_two, root_two, ln2_gain)
    d_ln2_gain = jnp.sum(grad_few * unit_two, axis=0)
    d_ln2_bias = jnp.sum(grad_few, axis=0)
    g_ffn = g_second.astype(BF16)
    d_b_down = jnp.sum(g_ffn.astype(F32), axis=0)

    def plane(values):
        values = jnp.concatenate([values, flip_tensor(values)], axis=0)
        values = jnp.concatenate([values, flip(values, 1)], axis=0)
        return jnp.concatenate([values, flip(values, 0)], axis=0)

    quarter = hidden_half // 4
    quarter_at = (lax.axis_index("dp") & 3) * quarter
    w_in_slice = lax.dynamic_slice_in_dim(w_in, quarter_at, quarter, 1)
    w_down_slice = lax.dynamic_slice_in_dim(w_down, quarter_at, quarter, 0)
    b_in_slice = lax.dynamic_slice_in_dim(b_in, quarter_at, quarter, 0)
    normed_plane = plane(normed_low)
    g_ffn_plane = plane(g_ffn)
    gate_plane, slope_plane = gelu_and_slope(mm(normed_plane, w_in_slice) + b_in_slice)
    d_w_down_slice = dot_tn(gate_plane.astype(BF16), g_ffn_plane)
    g_pre_plane = (slope_plane * dot_nt(g_ffn_plane, w_down_slice)).astype(BF16)
    d_w_in_slice = dot_tn(normed_plane, g_pre_plane)

    g_pre = [
        (gates[at][1] * dot_nt(g_ffn, w_down_both[at])).astype(BF16) for at in range(2)
    ]
    d_b_in = [jnp.sum(g.astype(F32), axis=0) for g in g_pre]
    g_normed = g_second + dot_nt(g_pre[0], w_in_both[0]) + dot_nt(g_pre[1], w_in_both[1])
    g_first = norm_back(g_normed, unit_one, root_one, ln1_gain)
    d_ln1_gain = jnp.sum(g_normed * unit_one, axis=0)
    d_ln1_bias = jnp.sum(g_normed, axis=0)
    g_branch = g_first.astype(BF16)
    d_b_out = jnp.sum(g_branch.astype(F32), axis=0)

    d_w_out, d_w_qkv, d_b_q, d_b_v, grads_qkv = [], [], [], [], []
    for at in range(2):
        d_w_out.append(dot_tn(context_few[at], g_branch))
        g_context = dot_nt(g_branch, w_out_both[at]).astype(BF16)
        dq, dk, dv = attend_back(queries_few[at], keys[at], values[at], g_context, seqs)
        d_b_q.append(jnp.sum(dq.astype(F32), axis=0))
        d_b_v.append(jnp.sum(dv.astype(F32), axis=0))
        d_w_qkv.append([dot_tn(tokens_few, dq), dot_tn(tokens, dk), dot_tn(tokens, dv)])
        grads_qkv.append((dq, dk, dv))

    chip_bits = list(range(2, bits))
    ffn_sums = []
    for local, axis in ((d_w_down_slice, 0), (d_w_in_slice, 1)):
        held = local
        for bit in chip_bits:
            held = scatter_sum(held, bit)
        held = spread(held, list(reversed(chip_bits)))
        for bit in (0, 1):
            held = in_order(held, flip(held, bit), bit, axis)
        ffn_sums.append(held.astype(F32))
    d_w_down, d_w_in = ffn_sums

    def whole_sum(own, other):
        own, other = scatter_sum(own, 0), scatter_sum(other, 0)
        held = own + flip_tensor(other.astype(BF16)).astype(F32)
        for bit in [1] + chip_bits:
            held = scatter_sum(held, bit)
        return spread(held, list(reversed(chip_bits)) + [1, 0]).astype(F32)

    d_w_out_sum = whole_sum(*d_w_out)
    d_w_qkv_sum = jnp.stack([whole_sum(d_w_qkv[0][i], d_w_qkv[1][i]) for i in range(3)], axis=1)

    def placed(parts):
        both = jnp.stack(parts)
        return jnp.where(half_at == 0, both, both[::-1]).reshape(-1)

    sections = [
        placed(d_b_q),
        placed(d_b_v),
        placed(d_b_in),
        d_b_out,
        d_ln1_gain,
        d_ln1_bias,
        d_b_down,
        d_ln2_gain,
        d_ln2_bias,
    ]
    small = jnp.concatenate(sections).reshape(-1, LANES)
    small = small + flip_tensor(small)
    for bit in range(bits):
        small = small + flip(small, bit)
    small = small.reshape(-1)
    cuts, at = [], 0
    for section in sections:
        cuts.append(small[at : at + section.size])
        at += section.size

    def own_half(vector):
        return lax.dynamic_index_in_dim(vector.reshape(2, -1), half_at, 0, keepdims=False)

    d_b_qv = jnp.stack([own_half(cuts[0]), own_half(cuts[1])])
    d_b_in_sum = own_half(cuts[2])

    few_back = g_first
    all_back = None
    for at in range(2):
        dq, dk, dv = grads_qkv[at]
        few_back = few_back + dot_nt(dq, w_qkv_both[at][0])
        part = dot_nt(dk, w_qkv_both[at][1]) + dot_nt(dv, w_qkv_both[at][2])
        all_back = part if all_back is None else all_back + part
    coarse = lax.reduce_precision(few_back, 8, 7)
    fine = (few_back - coarse).astype(BF16)
    pieces = jnp.concatenate(
        [coarse.astype(BF16).reshape(seqs, slots, width), fine.reshape(seqs, slots, width)], axis=1
    )
    spreading = jnp.concatenate([picks, picks], axis=1)
    d_tokens = all_back + jnp.einsum(
        "srt,srd->std", spreading, pieces, preferred_element_type=F32
    ).reshape(rows, width)

    branch = b_out
    for at in range(2):
        queries = (mm(tokens, w_qkv_both[at][0]) + b_q_both[at]).astype(BF16)
        context = attend(queries, keys[at], values[at], seqs)
        branch = branch + mm(context, w_out_both[at])
    unit, _ = norm_rows(tokens.astype(F32) + branch)
    normed = unit * ln1_gain + ln1_bias
    normed_bf = normed.astype(BF16)
    ffn_out = b_down
    for at in range(2):
        hidden = gelu(mm(normed_bf, w_in_both[at]) + b_in_both[at]).astype(BF16)
        ffn_out = ffn_out + mm(hidden, w_down_both[at])
    unit, _ = norm_rows(normed + ffn_out)
    mixed = (unit * ln2_gain + ln2_bias).astype(BF16)

    return (
        mixed,
        d_tokens,
        d_w_qkv_sum,
        d_b_qv,
        d_w_out_sum,
        cuts[3],
        cuts[4],
        cuts[5],
        d_w_in,
        d_b_in_sum,
        d_w_down,
        cuts[6],
        cuts[7],
        cuts[8],
    )


def solution(mesh):
    placed = (
        P(("dp", "tensor"), None),
        P(("dp", "tensor"), None),
        P("dp", None),
        P(None, None, "tensor"),
        P(None, "tensor"),
        P("tensor", None),
        P(),
        P(),
        P(),
        P(None, "tensor"),
        P("tensor"),
        P("tensor", None),
        P(),
        P(),
        P(),
    )
    return jax.shard_map(
        body,
        mesh=mesh,
        in_specs=placed,
        out_specs=(
            P(("dp", "tensor"), None),
            P(("dp", "tensor"), None),
            P(None, None, "tensor"),
            P(None, "tensor"),
            P("tensor", None),
            P(),
            P(),
            P(),
            P(None, "tensor"),
            P("tensor"),
            P("tensor", None),
            P(),
            P(),
            P(),
        ),
        check_vma=False,
    )
```

time: 966 us -> 522 us (0.54)
  waiting for transfers between devices: 605 us -> 160 us
  blocking collectives: 71.4 us -> 0 us
  starting transfers between devices: 1.16 us -> 65.9 us
  Pallas kernels: 0 us -> 43.9 us
  matrix products: 130 us -> 101 us
  between operations: 14.7 us -> 3.45 us
    reduce_scatter x4 -> x0, waiting for transfers between devices: 230 us -> none  [the longest x1 77.2 us: body(): lax.psum_scatter(jnp.einsum('rf,df->rd', rows_part, w_in, preferred_eleme...]
    psum x1 -> x0, waiting for transfers between devices: 194 us -> none  [body(): lax.psum((d_w_qkv, d_b_qv, d_w_out, d_b_out, d_ln1_gain, d_ln1_bias, d_w_...]
    all_gather x4 -> x0, waiting for transfers between devices: 180 us -> none  [the longest x1 45.3 us: body(): full_tokens = lax.all_gather(tokens, 'tensor', axis=0, tiled=True)]
    ppermute x0 -> x80, waiting for transfers between devices: none -> 160 us  [the longest x68 136 us: flip(): lax.ppermute(values, 'dp', [(at, at ^ 1 << bit) for at in range(size)])]
    psum x2 -> x0, blocking collectives: 71.4 us -> none  [the longest x1 64.1 us: body(): lax.psum((d_w_qkv, d_b_qv, d_w_out, d_b_out, d_ln1_gain, d_ln1_bias, d_w_...]
    ppermute x0 -> x80, starting transfers between devices: none -> 65.9 us  [the longest x68 53 us: flip(): lax.ppermute(values, 'dp', [(at, at ^ 1 << bit) for at in range(size)])]
    pallas_call x0 -> x6, Pallas kernels: none -> 43.9 us  [the longest x4 32.4 us: attend(): pl.pallas_call(attend_kernel, grid=(seqs, inner // LANES, tiles), in_spec...]
    dynamic_slice x9 -> x20, local copies, waits for them, and re-layouts: 4.91 us -> 35.1 us  [the longest x8 20.6 us: split_by(): keep = lax.dynamic_index_in_dim(halves, at, 0, keepdims=False)]
  transfers between devices with their start and end apart: 9 -> 80, of which waited for: 8 -> 41; matrix products, arithmetic and copies ran while one was open for 5% -> 45% of each run, Pallas kernels for 0% -> 8%
where the time goes in v1:
time: 522 us; the launch traced here: 517 us
  waiting for transfers between devices  160 us (31%)
  matrix products  101 us (19%)
  local copies, waits for them, and re-layouts  83.6 us (16%)
  starting transfers between devices  65.9 us (13%)
  other arithmetic  58.7 us (11%)
  Pallas kernels  43.9 us (8%)
    ppermute x68, waiting for transfers between devices, flip(): lax.ppermute(values, 'dp', [(at, at ^ 1 << bit) for at in range(size)])  136 us
    ppermute x68, starting transfers between devices, flip(): lax.ppermute(values, 'dp', [(at, at ^ 1 << bit) for at in range(size)])  53 us
    dot_general x19, matrix products, mm(): return jnp.dot(left, right, preferred_element_type=F32)  47.1 us
    pallas_call x4, Pallas kernels, attend(): pl.pallas_call(attend_kernel, grid=(seqs, inner // LANES, tiles), in_spec...  32.4 us
    dot_general x12, matrix products, dot_nt(): lax.dot_general(left, right, (((1,), (1,)), ((), ())), preferred_element_...  26.2 us
    unnamed x258, local copies, waits for them, and re-layouts  23.9 us
    ppermute x12, waiting for transfers between devices, flip_tensor(): return lax.ppermute(values, 'tensor', [(0, 1), (1, 0)])  23.9 us
    dot_general x10, matrix products, dot_tn(): lax.dot_general(left, right, (((0,), (0,)), ((), ())), preferred_element_...  22.8 us
  transfers between devices with their start and end apart: 80, of which 41 were waited for; matrix products, arithmetic and copies ran while one was open for 45% of the time, Pallas kernels for 8%

profile of v1, /device:TPU:0, one launch (start us, length us, event | category | flops | bytes accessed | tf_op | source)
XLA Modules:
  0.0 516.6 jit_solution(355668725209793895)
XLA Ops:
  2.5 2.9 collective-permute-start.13
  14.3 3.5 add_convert_fusion.4.q_ref
  23.0 12.5 %shard_map.254 = bf16[1024,384]{1,0:T(8,128)(2,1)S(1)} custom-call(bf16[1024,384]{1,0:T(8,128)(2,1)S(1)} %copy-done.23, bf16[1024,384]{1,0:T(8,128)(2,1)S(1)} %convolution_convert_fusion.1.k_ref, bf16[1024,384]{1,0:T(8,128)(2,1)S(1)} %copy-done.12), custom_call_target="tpu_custom_call" | custom-call | flops 3221225472 | bytes 3145728 | tf_op jit(solution)/shard_map/pallas_call | solution.py:106
  35.5 2.7 fusion.189
  42.7 3.6 shard_map.256
  48.3 2.5 multiply_reduce_fusion.9
  51.7 2.6 copy.53
  63.4 3.3 collective-permute-done.7
  71.7 5.2 %collective-permute-done.14 = bf16[192,768]{1,0:T(8,128)(2,1)S(1)} collective-permute-done((bf16[192,768]{1,0:T(8,128)(2,1)}, bf16[192,768]{1,0:T(8,128)(2,1)S(1)}, u32[]{:S(2)}, u32[]{:S(2)}) %collective-permute-start.14) | collective-permute-done | bytes 294944 | tf_op jit(solution)/shard_map/ppermute | solution.py:19
  81.7 4.7 collective-permute-done.2
  86.8 5.7 %collective-permute-done.15 = bf16[384,768]{1,0:T(8,128)(2,1)S(1)} collective-permute-done((bf16[384,768]{1,0:T(8,128)(2,1)S(1)}, bf16[384,768]{1,0:T(8,128)(2,1)S(1)}, u32[]{:S(2)}, u32[]{:S(2)}) %collective-permute-start.15) | collective-permute-done | bytes 589856 | tf_op jit(solution)/shard_map/ppermute | solution.py:19
  93.9 4.7 collective-permute-done.11
  105.0 12.3 %shard_map.255 = bf16[1024,384]{1,0:T(8,128)(2,1)S(1)} custom-call(bf16[1024,384]{1,0:T(8,128)(2,1)S(1)} %fusion.27.q_ref, bf16[1024,384]{1,0:T(8,128)(2,1)S(1)} %fusion.26.k_ref, bf16[1024,384]{1,0:T(8,128)(2,1)S(1)} %fusion.28.v_ref), custom_call_target="tpu_custom_call" | custom-call | flops 3221225472 | bytes 3145728 | tf_op jit(solution)/shard_map/pallas_call | solution.py:106
  119.2 4.0 shard_map.257
  124.7 10.7 %fusion.59 = f32[1024,768]{0,1:T(8,128)} fusion(bf16[1536,768]{1,0:T(8,128)(2,1)} %param.26, bf16[768,1536]{1,0:T(8,128)(2,1)S(1)} %copy-done, f32[1536]{0:T(1024)S(1)} %copy-done.91, f32[1024,768]{0,1:T(8,128)} %copy-done.31, f32[768]{0:T(1024)S(1)} %copy-done.110, f32[768]{0:T(1024)S(1)} %copy-done.94, f32[1024]{0:T(1024)S(1)} %add_rsqrt_fusion.1, ...), kind=kOutput, calls=%fused_computation.129 | convolution fusion | flops 4851499008 | bytes 11030528 | tf_op jit(solution)/shard_map/dot_general | solution.py:183
  139.0 5.1 collective-permute-done.62
  155.2 2.7 convert_reduce_fusion.3
  157.9 2.9 convert_reduce_fusion.2
  166.0 5.7 %shard_map.258 = (bf16[160,384]{1,0:T(8,128)(2,1)S(1)}, bf16[1024,384]{1,0:T(8,128)(2,1)S(1)}, bf16[1024,384]{1,0:T(8,128)(2,1)S(1)}) custom-call(bf16[160,384]{1,0:T(8,128)(2,1)S(1)} %copy-done.20, bf16[1024,384]{1,0:T(8,128)(2,1)S(1)} %copy-done.11, bf16[1024,384]{1,0:T(8,128)(2,1)S(1)} %copy-done.14, bf16[160,384]{1,0:T(8,128)(2,1)S(1)} %convolution_convert_fusion.4.g_ref), custom_call_target="tpu_custom_call" | custom-call | flops 1258291200 | bytes 3514368 | tf_op jit(solution)/shard_map/pallas_call | solution.py:139
  171.7 4.0 fusion.76
  177.6 5.7 %shard_map.259 = (bf16[160,384]{1,0:T(8,128)(2,1)S(1)}, bf16[1024,384]{1,0:T(8,128)(2,1)S(1)}, bf16[1024,384]{1,0:T(8,128)(2,1)S(1)}) custom-call(bf16[160,384]{1,0:T(8,128)(2,1)S(1)} %copy-done.22, bf16[1024,384]{1,0:T(8,128)(2,1)S(1)} %copy-done.16, bf16[1024,384]{1,0:T(8,128)(2,1)S(1)} %copy-done.18, bf16[160,384]{1,0:T(8,128)(2,1)S(1)} %convolution_convert_fusion.3.g_ref), custom_call_target="tpu_custom_call" | custom-call | flops 1258291200 | bytes 3514368 | tf_op jit(solution)/shard_map/pallas_call | solution.py:139
  183.3 2.7 fusion.77
  187.9 2.8 reshape.432
  190.7 2.8 reshape.433
  193.5 2.8 constant_dynamic-slice_fusion.6
  196.3 2.7 constant_dynamic-slice_fusion.4
  201.7 3.9 fusion.75
  209.2 2.9 reshape.428
  212.1 2.6 constant_dynamic-slice_fusion.8
  214.7 2.7 constant_dynamic-slice_fusion.7
  217.4 3.2 reshape.427
  220.6 2.6 constant_dynamic-slice_fusion.10
  223.3 2.6 constant_dynamic-slice_fusion.9
  235.0 13.7 %fusion.184 = (f32[1024]{0:T(1024)S(1)}, f32[1024,768]{0,1:T(8,128)}) fusion(bf16[768,768]{1,0:T(8,128)(2,1)} %copy-done.76, bf16[768,768]{1,0:T(8,128)(2,1)} %copy-done.75, f32[1536]{0:T(1024)S(1)} %copy-done.109, bf16[384,1536]{1,0:T(8,128)(2,1)} %copy-done.74, bf16[384,1536]{1,0:T(8,128)(2,1)} %copy-done.73, f32[1024,768]{0,1:T(8,128)} %copy-done.31, ...), kind=kOutput, calls=%fused_computation.474 | convolution fusion | flops 4867226624 | bytes 14183424 | tf_op jit(solution)/shard_map/dot_general | solution.py:183
  255.7 3.7 add_convert_fusion
  260.9 5.1 bitcast_add_fusion
  270.3 2.6 copy.69
  273.0 3.0 copy.67
  275.9 2.8 copy.76
  293.3 2.9 copy.63
  296.2 2.8 copy.74
  299.0 2.9 copy.73
  302.0 2.7 collective-permute-start.51
  317.5 6.5 %collective-permute-done.39 = bf16[384,384]{1,0:T(8,128)(2,1)S(1)} collective-permute-done((bf16[384,384]{1,0:T(8,128)(2,1)S(1)}, bf16[384,384]{1,0:T(8,128)(2,1)S(1)}, u32[]{:S(2)}, u32[]{:S(2)}) %collective-permute-start.39) | collective-permute-done | bytes 294944 | tf_op jit(solution)/shard_map/ppermute | solution.py:23
  325.8 4.6 collective-permute-done.29
  332.2 4.5 collective-permute-done.19
  339.0 3.2 collective-permute-done.54
  343.5 4.2 collective-permute-done.40
  385.2 2.7 collective-permute-done.45
  394.7 3.5 convolution_add_fusion
  399.2 6.6 %fusion.33 = f32[768,384]{1,0:T(8,128)} fusion(f32[1280,384]{1,0:T(8,128)} %convolution_add_fusion, bf16[1536,768]{1,0:T(8,128)(2,1)} %param.26, s32[]{:T(128)S(6)} %select_n.585, bf16[640,768]{1,0:T(8,128)(2,1)} %collective-permute-done.67, bf16[320,768]{1,0:T(8,128)(2,1)} %copy-done.84, bf16[160,768]{1,0:T(8,128)(2,1)} %collective-permute-done.65, ...), kind=kOutput, calls=%fused_computation.80 | convolution fusion | flops 1535016960 | bytes 7667716 | tf_op jit(solution)/shard_map/dot_general | solution.py:77
  407.7 3.1 fusion.48
  412.3 4.6 collective-permute-done.68
  417.7 7.9 %collective-permute-done.74 = bf16[192,768]{1,0:T(8,128)(2,1)S(1)} collective-permute-done((bf16[192,768]{1,0:T(8,128)(2,1)S(1)}, bf16[192,768]{1,0:T(8,128)(2,1)S(1)}, u32[]{:S(2)}, u32[]{:S(2)}) %collective-permute-start.74) | collective-permute-done | bytes 294944 | tf_op jit(solution)/shard_map/ppermute | solution.py:19
  428.7 8.6 %collective-permute-done.75 = bf16[96,768]{1,0:T(8,128)(2,1)S(1)} collective-permute-done((bf16[96,768]{1,0:T(8,128)(2,1)S(1)}, bf16[96,768]{1,0:T(8,128)(2,1)S(1)}, u32[]{:S(2)}, u32[]{:S(2)}) %collective-permute-start.75) | collective-permute-done | bytes 147488 | tf_op jit(solution)/shard_map/ppermute | solution.py:19
  437.4 3.0 collective-permute-done.70
  440.5 2.6 collective-permute-start.71
  443.0 3.8 collective-permute-done.76
  446.9 6.2 %collective-permute-done.71 = bf16[384,384]{1,0:T(8,128)(2,1)S(1)} collective-permute-done((bf16[384,384]{1,0:T(8,128)(2,1)S(1)}, bf16[384,384]{1,0:T(8,128)(2,1)S(1)}, u32[]{:S(2)}, u32[]{:S(2)}) %collective-permute-start.71) | collective-permute-done | bytes 294944 | tf_op jit(solution)/shard_map/ppermute | solution.py:19
  454.5 4.4 collective-permute-done.77
  467.5 21.0 %collective-permute-done.73 = bf16[768,768]{1,0:T(8,128)(2,1)S(1)} collective-permute-done((bf16[768,768]{1,0:T(8,128)(2,1)S(1)}, bf16[768,768]{1,0:T(8,128)(2,1)S(1)}, u32[]{:S(2)}, u32[]{:S(2)}) %collective-permute-start.73) | collective-permute-done | bytes 1179680 | tf_op jit(solution)/shard_map/ppermute | solution.py:19
  489.0 2.8 maximum_convert_fusion
  491.8 21.6 %collective-permute-done.79 = bf16[768,768]{1,0:T(8,128)(2,1)S(1)} collective-permute-done((bf16[768,768]{1,0:T(8,128)(2,1)S(1)}, bf16[768,768]{1,0:T(8,128)(2,1)S(1)}, u32[]{:S(2)}, u32[]{:S(2)}) %collective-permute-start.79) | collective-permute-done | bytes 1179680 | tf_op jit(solution)/shard_map/ppermute | solution.py:19
  513.9 2.5 maximum_convert_fusion.1
  (621 shorter events, 201.9 us)
Async XLA Ops:
  2.5 64.3 %collective-permute-start.13 = (bf16[192,768]{1,0:T(8,128)(2,1)}, bf16[192,768]{1,0:T(8,128)(2,1)}, u32[]{:S(2)}, u32[]{:S(2)}) collective-permute-start(bf16[192,768]{1,0:T(8,128)(2,1)} %constant_dynamic-slice_fusion.12), channel_id=1, source_target_pairs={{0,1},{1,0},{2,3},{3,2},{4,5},{5,4},{6,7},{7,6},{8,9},{9,8},{10,11... | collective-permute-start | bytes 884744 | tf_op jit(solution)/shard_map/ppermute | solution.py:23
  7.0 49.7 %collective-permute-start.4 = (f32[18,128]{1,0:T(8,128)S(1)}, f32[18,128]{1,0:T(8,128)}, u32[]{:S(2)}, u32[]{:S(2)}) collective-permute-start(f32[18,128]{1,0:T(8,128)S(1)} %maximum_bitcast_fusion), channel_id=1, source_target_pairs={{0,1},{1,0},{2,3},{3,2},{4,5},{5,4},{6,7},{7,6},{8,9},{9,8},{10,11... | collective-permute-start | bytes 27656 | tf_op jit(solution)/shard_map/ppermute | solution.py:23
  7.7 60.8 %collective-permute-start.9 = (bf16[96,1536]{1,0:T(8,128)(2,1)}, bf16[96,1536]{1,0:T(8,128)(2,1)}, u32[]{:S(2)}, u32[]{:S(2)}) collective-permute-start(bf16[96,1536]{1,0:T(8,128)(2,1)} %constant_dynamic-slice_fusion.13), channel_id=1, source_target_pairs={{0,1},{1,0},{2,3},{3,2},{4,5},{5,4},{6,7},{7,6},{8,9},{9,8},{10,11... | collective-permute-start | bytes 884744 | tf_op jit(solution)/shard_map/ppermute | solution.py:23
  11.4 51.5 %collective-permute-start = (bf16[288,384]{1,0:T(8,128)(2,1)}, bf16[288,384]{1,0:T(8,128)(2,1)}, u32[]{:S(2)}, u32[]{:S(2)}) collective-permute-start(bf16[288,384]{1,0:T(8,128)(2,1)} %constant_dynamic-slice_fusion.15), channel_id=1, source_target_pairs={{0,1},{1,0},{2,3},{3,2},{4,5},{5,4},{6,7},{7,6},{8,9},{9,8},{10,11... | collective-permute-start | bytes 663560 | tf_op jit(solution)/shard_map/ppermute | solution.py:23
  12.3 42.8 %collective-permute-start.5 = (bf16[48,768]{1,0:T(8,128)(2,1)S(1)}, bf16[48,768]{1,0:T(8,128)(2,1)}, u32[]{:S(2)}, u32[]{:S(2)}) collective-permute-start(bf16[48,768]{1,0:T(8,128)(2,1)S(1)} %constant_dynamic-slice_fusion.14), channel_id=1, source_target_pairs={{0,1},{1,0},{2,3},{3,2},{4,5},{5,4},{6,7},{7,6},{8,9},{9,8},{10,11... | collective-permute-start | bytes 221192 | tf_op jit(solution)/shard_map/ppermute | solution.py:23
  60.5 6.1 %collective-permute-start.7 = (bf16[96,768]{1,0:T(8,128)(2,1)S(1)}, bf16[96,768]{1,0:T(8,128)(2,1)S(1)}, u32[]{:S(2)}, u32[]{:S(2)}) collective-permute-start(bf16[96,768]{1,0:T(8,128)(2,1)S(1)} %pad_maximum_fusion.42), channel_id=1, source_target_pairs={{0,4},{2,6},{4,0},{6,2},{8,12},{10,14},{12,8},{14,10},{16,20},{18,... | collective-permute-start | bytes 442376 | tf_op jit(solution)/shard_map/ppermute | solution.py:19
  62.9 6.5 %collective-permute-start.1 = (bf16[288,384]{1,0:T(8,128)(2,1)}, bf16[288,384]{1,0:T(8,128)(2,1)S(1)}, u32[]{:S(2)}, u32[]{:S(2)}) collective-permute-start(bf16[288,384]{1,0:T(8,128)(2,1)} %collective-permute-done), channel_id=1, source_target_pairs={{0,4},{2,6},{4,0},{6,2},{8,12},{10,14},{12,8},{14,10},{16,20},{18,... | collective-permute-start | bytes 663560 | tf_op jit(solution)/shard_map/ppermute | solution.py:19
  66.7 14.9 %collective-permute-start.8 = (bf16[192,768]{1,0:T(8,128)(2,1)S(1)}, bf16[192,768]{1,0:T(8,128)(2,1)S(1)}, u32[]{:S(2)}, u32[]{:S(2)}) collective-permute-start(bf16[192,768]{1,0:T(8,128)(2,1)S(1)} %pad_maximum_fusion.32), channel_id=1, source_target_pairs={{0,2},{2,0},{4,6},{6,4},{8,10},{10,8},{12,14},{14,12},{16,18},{18,... | collective-permute-start | bytes 884744 | tf_op jit(solution)/shard_map/ppermute | solution.py:19
  66.8 10.1 %collective-permute-start.14 = (bf16[192,768]{1,0:T(8,128)(2,1)}, bf16[192,768]{1,0:T(8,128)(2,1)S(1)}, u32[]{:S(2)}, u32[]{:S(2)}) collective-permute-start(bf16[192,768]{1,0:T(8,128)(2,1)} %collective-permute-done.13), channel_id=1, source_target_pairs={{0,8},{2,10},{4,12},{6,14},{8,0},{10,2},{12,4},{14,6},{16,24},{18,... | collective-permute-start | bytes 884744 | tf_op jit(solution)/shard_map/ppermute | solution.py:19
  68.5 10.5 %collective-permute-start.10 = (bf16[96,1536]{1,0:T(8,128)(2,1)}, bf16[96,1536]{1,0:T(8,128)(2,1)S(1)}, u32[]{:S(2)}, u32[]{:S(2)}) collective-permute-start(bf16[96,1536]{1,0:T(8,128)(2,1)} %collective-permute-done.9), channel_id=1, source_target_pairs={{0,4},{2,6},{4,0},{6,2},{8,12},{10,14},{12,8},{14,10},{16,20},{18,... | collective-permute-start | bytes 884744 | tf_op jit(solution)/shard_map/ppermute | solution.py:19
  70.4 16.0 %collective-permute-start.2 = (bf16[576,384]{1,0:T(8,128)(2,1)S(1)}, bf16[576,384]{1,0:T(8,128)(2,1)S(1)}, u32[]{:S(2)}, u32[]{:S(2)}) collective-permute-start(bf16[576,384]{1,0:T(8,128)(2,1)S(1)} %pad_maximum_fusion.26), channel_id=1, source_target_pairs={{0,8},{2,10},{4,12},{6,14},{8,0},{10,2},{12,4},{14,6},{16,24},{18,... | collective-permute-start | bytes 1327112 | tf_op jit(solution)/shard_map/ppermute | solution.py:19
  78.0 14.5 %collective-permute-start.15 = (bf16[384,768]{1,0:T(8,128)(2,1)S(1)}, bf16[384,768]{1,0:T(8,128)(2,1)S(1)}, u32[]{:S(2)}, u32[]{:S(2)}) collective-permute-start(bf16[384,768]{1,0:T(8,128)(2,1)S(1)} %pad_maximum_fusion.21), channel_id=1, source_target_pairs={{0,4},{2,6},{4,0},{6,2},{8,12},{10,14},{12,8},{14,10},{16,20},{18,... | collective-permute-start | bytes 1769480 | tf_op jit(solution)/shard_map/ppermute | solution.py:19
  80.0 18.6 %collective-permute-start.11 = (bf16[192,1536]{1,0:T(8,128)(2,1)S(1)}, bf16[192,1536]{1,0:T(8,128)(2,1)S(1)}, u32[]{:S(2)}, u32[]{:S(2)}) collective-permute-start(bf16[192,1536]{1,0:T(8,128)(2,1)S(1)} %pad_maximum_fusion.20), channel_id=1, source_target_pairs={{0,8},{2,10},{4,12},{6,14},{8,0},{10,2},{12,4},{14,6},{16,24},{18,... | collective-permute-start | bytes 1769480 | tf_op jit(solution)/shard_map/ppermute | solution.py:19
  86.7 13.3 %collective-permute-start.3 = (bf16[1152,384]{1,0:T(8,128)(2,1)S(1)}, bf16[1152,384]{1,0:T(8,128)(2,1)S(1)}, u32[]{:S(2)}, u32[]{:S(2)}) collective-permute-start(bf16[1152,384]{1,0:T(8,128)(2,1)S(1)} %pad_maximum_fusion.10), channel_id=1, source_target_pairs={{0,2},{2,0},{4,6},{6,4},{8,10},{10,8},{12,14},{14,12},{16,18},{18,... | collective-permute-start | bytes 2654216 | tf_op jit(solution)/shard_map/ppermute | solution.py:19
  93.9 54.3 %collective-permute-start.16 = (bf16[768,768]{1,0:T(8,128)(2,1)}, bf16[768,768]{1,0:T(8,128)(2,1)}, u32[]{:S(2)}, u32[]{:S(2)}) collective-permute-start(bf16[768,768]{1,0:T(8,128)(2,1)} %pad_maximum_fusion.5), channel_id=1, source_target_pairs={{0,2},{2,0},{4,6},{6,4},{8,10},{10,8},{12,14},{14,12},{16,18},{18,... | collective-permute-start | bytes 3538952 | tf_op jit(solution)/shard_map/ppermute | solution.py:19
  100.0 45.9 %collective-permute-start.12 = (bf16[384,1536]{1,0:T(8,128)(2,1)}, bf16[384,1536]{1,0:T(8,128)(2,1)}, u32[]{:S(2)}, u32[]{:S(2)}) collective-permute-start(bf16[384,1536]{1,0:T(8,128)(2,1)} %pad_maximum_fusion.4), channel_id=1, source_target_pairs={{0,2},{2,0},{4,6},{6,4},{8,10},{10,8},{12,14},{14,12},{16,18},{18,... | collective-permute-start | bytes 3538952 | tf_op jit(solution)/shard_map/ppermute | solution.py:19
  136.6 7.6 %collective-permute-start.62 = (bf16[160,768]{1,0:T(8,128)(2,1)S(1)}, bf16[160,768]{1,0:T(8,128)(2,1)S(1)}, u32[]{:S(2)}, u32[]{:S(2)}) collective-permute-start(bf16[160,768]{1,0:T(8,128)(2,1)S(1)} %fusion.96), channel_id=1, source_target_pairs={{0,1},{1,0},{2,3},{3,2},{4,5},{5,4},{6,7},{7,6},{8,9},{9,8},{10,11... | collective-permute-start | bytes 737288 | tf_op jit(solution)/shard_map/ppermute | solution.py:23
  145.0 157.0 %collective-permute-start.63 = (bf16[320,768]{1,0:T(8,128)(2,1)}, bf16[320,768]{1,0:T(8,128)(2,1)}, u32[]{:S(2)}, u32[]{:S(2)}) collective-permute-start(bf16[320,768]{1,0:T(8,128)(2,1)} %pad_maximum_fusion.24), channel_id=1, source_target_pairs={{0,4},{2,6},{4,0},{6,2},{8,12},{10,14},{12,8},{14,10},{16,20},{18,... | collective-permute-start | bytes 1474568 | tf_op jit(solution)/shard_map/ppermute | solution.py:19
  234.4 75.1 %collective-permute-start.65 = (bf16[160,768]{1,0:T(8,128)(2,1)}, bf16[160,768]{1,0:T(8,128)(2,1)}, u32[]{:S(2)}, u32[]{:S(2)}) collective-permute-start(bf16[160,768]{1,0:T(8,128)(2,1)} %get-tuple-element.79), channel_id=1, source_target_pairs={{0,1},{1,0},{2,3},{3,2},{4,5},{5,4},{6,7},{7,6},{8,9},{9,8},{10,11... | collective-permute-start | bytes 737288 | tf_op jit(solution)/shard_map/ppermute | solution.py:23
  254.1 13.8 %collective-permute-start.47 = (f32[72,128]{1,0:T(8,128)S(1)}, f32[72,128]{1,0:T(8,128)S(1)}, u32[]{:S(2)}, u32[]{:S(2)}) collective-permute-start(f32[72,128]{1,0:T(8,128)S(1)} %bitcast.352), channel_id=1, source_target_pairs={{0,1},{1,0},{2,3},{3,2},{4,5},{5,4},{6,7},{7,6},{8,9},{9,8},{10,11... | collective-permute-start | bytes 110600 | tf_op jit(solution)/shard_map/ppermute | solution.py:23
  268.5 12.5 %collective-permute-start.48 = (f32[72,128]{1,0:T(8,128)}, f32[72,128]{1,0:T(8,128)}, u32[]{:S(2)}, u32[]{:S(2)}) collective-permute-start(f32[72,128]{1,0:T(8,128)} %bitcast_add_fusion.25), channel_id=1, source_target_pairs={{0,2},{2,0},{4,6},{6,4},{8,10},{10,8},{12,14},{14,12},{16,18},{18,... | collective-permute-start | bytes 110600 | tf_op jit(solution)/shard_map/ppermute | solution.py:19
  278.7 32.4 %collective-permute-start.38 = (bf16[384,384]{1,0:T(8,128)(2,1)}, bf16[384,384]{1,0:T(8,128)(2,1)}, u32[]{:S(2)}, u32[]{:S(2)}) collective-permute-start(bf16[384,384]{1,0:T(8,128)(2,1)} %bitcast.350), channel_id=1, source_target_pairs={{0,2},{2,0},{4,6},{6,4},{8,10},{10,8},{12,14},{14,12},{16,18},{18,... | collective-permute-start | bytes 884744 | tf_op jit(solution)/shard_map/ppermute | solution.py:19
  281.0 35.0 %collective-permute-start.37 = (bf16[384,384]{1,0:T(8,128)(2,1)}, bf16[384,384]{1,0:T(8,128)(2,1)}, u32[]{:S(2)}, u32[]{:S(2)}) collective-permute-start(bf16[384,384]{1,0:T(8,128)(2,1)} %bitcast.349), channel_id=1, source_target_pairs={{0,2},{2,0},{4,6},{6,4},{8,10},{10,8},{12,14},{14,12},{16,18},{18,... | collective-permute-start | bytes 884744 | tf_op jit(solution)/shard_map/ppermute | solution.py:19
  285.8 16.1 %collective-permute-start.50 = (f32[72,128]{1,0:T(8,128)S(1)}, f32[72,128]{1,0:T(8,128)S(1)}, u32[]{:S(2)}, u32[]{:S(2)}) collective-permute-start(f32[72,128]{1,0:T(8,128)S(1)} %add.645), channel_id=1, source_target_pairs={{0,8},{2,10},{4,12},{6,14},{8,0},{10,2},{12,4},{14,6},{16,24},{18,... | collective-permute-start | bytes 110600 | tf_op jit(solution)/shard_map/ppermute | solution.py:19
  301.9 12.9 %collective-permute-start.28 = (bf16[384,384]{1,0:T(8,128)(2,1)}, bf16[384,384]{1,0:T(8,128)(2,1)}, u32[]{:S(2)}, u32[]{:S(2)}) collective-permute-start(bf16[384,384]{1,0:T(8,128)(2,1)} %bitcast.351), channel_id=1, source_target_pairs={{0,2},{2,0},{4,6},{6,4},{8,10},{10,8},{12,14},{14,12},{16,18},{18,... | collective-permute-start | bytes 884744 | tf_op jit(solution)/shard_map/ppermute | solution.py:19
  307.5 18.1 %collective-permute-start.27 = (bf16[384,384]{1,0:T(8,128)(2,1)}, bf16[384,384]{1,0:T(8,128)(2,1)S(1)}, u32[]{:S(2)}, u32[]{:S(2)}) collective-permute-start(bf16[384,384]{1,0:T(8,128)(2,1)} %bitcast.242), channel_id=1, source_target_pairs={{0,2},{2,0},{4,6},{6,4},{8,10},{10,8},{12,14},{14,12},{16,18},{18,... | collective-permute-start | bytes 884744 | tf_op jit(solution)/shard_map/ppermute | solution.py:19
  312.5 19.1 %collective-permute-start.17 = (bf16[384,384]{1,0:T(8,128)(2,1)S(1)}, bf16[384,384]{1,0:T(8,128)(2,1)S(1)}, u32[]{:S(2)}, u32[]{:S(2)}) collective-permute-start(bf16[384,384]{1,0:T(8,128)(2,1)S(1)} %copy-done.86), channel_id=1, source_target_pairs={{0,2},{2,0},{4,6},{6,4},{8,10},{10,8},{12,14},{14,12},{16,18},{18,... | collective-permute-start | bytes 884744 | tf_op jit(solution)/shard_map/ppermute | solution.py:19
  314.1 9.9 %collective-permute-start.39 = (bf16[384,384]{1,0:T(8,128)(2,1)S(1)}, bf16[384,384]{1,0:T(8,128)(2,1)S(1)}, u32[]{:S(2)}, u32[]{:S(2)}) collective-permute-start(bf16[384,384]{1,0:T(8,128)(2,1)S(1)} %fusion.66), channel_id=1, source_target_pairs={{0,1},{1,0},{2,3},{3,2},{4,5},{5,4},{6,7},{7,6},{8,9},{9,8},{10,11... | collective-permute-start | bytes 884744 | tf_op jit(solution)/shard_map/ppermute | solution.py:23
  314.8 23.2 %collective-permute-start.52 = (bf16[192,768]{1,0:T(8,128)(2,1)S(1)}, bf16[192,768]{1,0:T(8,128)(2,1)S(1)}, u32[]{:S(2)}, u32[]{:S(2)}) collective-permute-start(bf16[192,768]{1,0:T(8,128)(2,1)S(1)} %copy-done.87), channel_id=1, source_target_pairs={{0,2},{2,0},{4,6},{6,4},{8,10},{10,8},{12,14},{14,12},{16,18},{18,... | collective-permute-start | bytes 884744 | tf_op jit(solution)/shard_map/ppermute | solution.py:19
  315.9 14.4 %collective-permute-start.29 = (bf16[384,384]{1,0:T(8,128)(2,1)S(1)}, bf16[384,384]{1,0:T(8,128)(2,1)S(1)}, u32[]{:S(2)}, u32[]{:S(2)}) collective-permute-start(bf16[384,384]{1,0:T(8,128)(2,1)S(1)} %fusion.68), channel_id=1, source_target_pairs={{0,1},{1,0},{2,3},{3,2},{4,5},{5,4},{6,7},{7,6},{8,9},{9,8},{10,11... | collective-permute-start | bytes 884744 | tf_op jit(solution)/shard_map/ppermute | solution.py:23
  324.1 12.6 %collective-permute-start.19 = (bf16[384,384]{1,0:T(8,128)(2,1)S(1)}, bf16[384,384]{1,0:T(8,128)(2,1)S(1)}, u32[]{:S(2)}, u32[]{:S(2)}) collective-permute-start(bf16[384,384]{1,0:T(8,128)(2,1)S(1)} %fusion.70), channel_id=1, source_target_pairs={{0,1},{1,0},{2,3},{3,2},{4,5},{5,4},{6,7},{7,6},{8,9},{9,8},{10,11... | collective-permute-start | bytes 884744 | tf_op jit(solution)/shard_map/ppermute | solution.py:23
  325.7 68.5 %collective-permute-start.64 = (bf16[640,768]{1,0:T(8,128)(2,1)S(1)}, bf16[640,768]{1,0:T(8,128)(2,1)S(1)}, u32[]{:S(2)}, u32[]{:S(2)}) collective-permute-start(bf16[640,768]{1,0:T(8,128)(2,1)S(1)} %copy-done.79), channel_id=1, source_target_pairs={{0,2},{2,0},{4,6},{6,4},{8,10},{10,8},{12,14},{14,12},{16,18},{18,... | collective-permute-start | bytes 2949128 | tf_op jit(solution)/shard_map/ppermute | solution.py:19
  330.4 24.8 %collective-permute-start.66 = (bf16[320,768]{1,0:T(8,128)(2,1)S(1)}, bf16[320,768]{1,0:T(8,128)(2,1)S(1)}, u32[]{:S(2)}, u32[]{:S(2)}) collective-permute-start(bf16[320,768]{1,0:T(8,128)(2,1)S(1)} %pad_maximum_fusion.25), channel_id=1, source_target_pairs={{0,4},{2,6},{4,0},{6,2},{8,12},{10,14},{12,8},{14,10},{16,20},{18,... | collective-permute-start | bytes 1474568 | tf_op jit(solution)/shard_map/ppermute | solution.py:19
  331.6 10.5 %collective-permute-start.54 = (bf16[192,768]{1,0:T(8,128)(2,1)S(1)}, bf16[192,768]{1,0:T(8,128)(2,1)S(1)}, u32[]{:S(2)}, u32[]{:S(2)}) collective-permute-start(bf16[192,768]{1,0:T(8,128)(2,1)S(1)} %fusion.64), channel_id=1, source_target_pairs={{0,1},{1,0},{2,3},{3,2},{4,5},{5,4},{6,7},{7,6},{8,9},{9,8},{10,11... | collective-permute-start | bytes 884744 | tf_op jit(solution)/shard_map/ppermute | solution.py:23
  336.7 11.0 %collective-permute-start.40 = (bf16[192,384]{1,0:T(8,128)(2,1)S(1)}, bf16[192,384]{1,0:T(8,128)(2,1)S(1)}, u32[]{:S(2)}, u32[]{:S(2)}) collective-permute-start(bf16[192,384]{1,0:T(8,128)(2,1)S(1)} %fusion.116), channel_id=1, source_target_pairs={{0,4},{2,6},{4,0},{6,2},{8,12},{10,14},{12,8},{14,10},{16,20},{18,... | collective-permute-start | bytes 442376 | tf_op jit(solution)/shard_map/ppermute | solution.py:19
  338.0 12.8 %collective-permute-start.30 = (bf16[192,384]{1,0:T(8,128)(2,1)S(1)}, bf16[192,384]{1,0:T(8,128)(2,1)S(1)}, u32[]{:S(2)}, u32[]{:S(2)}) collective-permute-start(bf16[192,384]{1,0:T(8,128)(2,1)S(1)} %fusion.115), channel_id=1, source_target_pairs={{0,4},{2,6},{4,0},{6,2},{8,12},{10,14},{12,8},{14,10},{16,20},{18,... | collective-permute-start | bytes 442376 | tf_op jit(solution)/shard_map/ppermute | solution.py:19
  342.2 10.8 %collective-permute-start.20 = (bf16[192,384]{1,0:T(8,128)(2,1)S(1)}, bf16[192,384]{1,0:T(8,128)(2,1)S(1)}, u32[]{:S(2)}, u32[]{:S(2)}) collective-permute-start(bf16[192,384]{1,0:T(8,128)(2,1)S(1)} %fusion.114), channel_id=1, source_target_pairs={{0,4},{2,6},{4,0},{6,2},{8,12},{10,14},{12,8},{14,10},{16,20},{18,... | collective-permute-start | bytes 442376 | tf_op jit(solution)/shard_map/ppermute | solution.py:19
  347.7 6.9 %collective-permute-start.55 = (bf16[96,768]{1,0:T(8,128)(2,1)S(1)}, bf16[96,768]{1,0:T(8,128)(2,1)S(1)}, u32[]{:S(2)}, u32[]{:S(2)}) collective-permute-start(bf16[96,768]{1,0:T(8,128)(2,1)S(1)} %fusion.117), channel_id=1, source_target_pairs={{0,4},{2,6},{4,0},{6,2},{8,12},{10,14},{12,8},{14,10},{16,20},{18,... | collective-permute-start | bytes 442376 | tf_op jit(solution)/shard_map/ppermute | solution.py:19
  350.9 7.0 %collective-permute-start.41 = (bf16[96,384]{1,0:T(8,128)(2,1)S(1)}, bf16[96,384]{1,0:T(8,128)(2,1)S(1)}, u32[]{:S(2)}, u32[]{:S(2)}) collective-permute-start(bf16[96,384]{1,0:T(8,128)(2,1)S(1)} %fusion.124), channel_id=1, source_target_pairs={{0,8},{2,10},{4,12},{6,14},{8,0},{10,2},{12,4},{14,6},{16,24},{18,... | collective-permute-start | bytes 221192 | tf_op jit(solution)/shard_map/ppermute | solution.py:19
  355.2 5.9 %collective-permute-start.56 = (bf16[48,768]{1,0:T(8,128)(2,1)S(1)}, bf16[48,768]{1,0:T(8,128)(2,1)S(1)}, u32[]{:S(2)}, u32[]{:S(2)}) collective-permute-start(bf16[48,768]{1,0:T(8,128)(2,1)S(1)} %fusion.125), channel_id=1, source_target_pairs={{0,8},{2,10},{4,12},{6,14},{8,0},{10,2},{12,4},{14,6},{16,24},{18,... | collective-permute-start | bytes 221192 | tf_op jit(solution)/shard_map/ppermute | solution.py:19
  357.9 41.3 %collective-permute-start.67 = (bf16[640,768]{1,0:T(8,128)(2,1)S(1)}, bf16[640,768]{1,0:T(8,128)(2,1)}, u32[]{:S(2)}, u32[]{:S(2)}) collective-permute-start(bf16[640,768]{1,0:T(8,128)(2,1)S(1)} %pad_maximum_fusion.9), channel_id=1, source_target_pairs={{0,2},{2,0},{4,6},{6,4},{8,10},{10,8},{12,14},{14,12},{16,18},{18,... | collective-permute-start | bytes 2949128 | tf_op jit(solution)/shard_map/ppermute | solution.py:19
  360.2 6.9 %collective-permute-start.32 = (bf16[48,384]{1,0:T(8,128)(2,1)S(1)}, bf16[48,384]{1,0:T(8,128)(2,1)S(1)}, u32[]{:S(2)}, u32[]{:S(2)}) collective-permute-start(bf16[48,384]{1,0:T(8,128)(2,1)S(1)} %fusion.131), channel_id=1, source_target_pairs={{0,16},{2,18},{4,20},{6,22},{8,24},{10,26},{12,28},{14,30},{16,0},... | collective-permute-start | bytes 110600 | tf_op jit(solution)/shard_map/ppermute | solution.py:19
  361.2 6.6 %collective-permute-start.22 = (bf16[48,384]{1,0:T(8,128)(2,1)S(1)}, bf16[48,384]{1,0:T(8,128)(2,1)S(1)}, u32[]{:S(2)}, u32[]{:S(2)}) collective-permute-start(bf16[48,384]{1,0:T(8,128)(2,1)S(1)} %fusion.130), channel_id=1, source_target_pairs={{0,16},{2,18},{4,20},{6,22},{8,24},{10,26},{12,28},{14,30},{16,0},... | collective-permute-start | bytes 110600 | tf_op jit(solution)/shard_map/ppermute | solution.py:19
  363.6 6.4 %collective-permute-start.57 = (bf16[24,768]{1,0:T(8,128)(2,1)S(1)}, bf16[24,768]{1,0:T(8,128)(2,1)S(1)}, u32[]{:S(2)}, u32[]{:S(2)}) collective-permute-start(bf16[24,768]{1,0:T(8,128)(2,1)S(1)} %fusion.133), channel_id=1, source_target_pairs={{0,16},{2,18},{4,20},{6,22},{8,24},{10,26},{12,28},{14,30},{16,0},... | collective-permute-start | bytes 110600 | tf_op jit(solution)/shard_map/ppermute | solution.py:19
  367.0 6.1 %collective-permute-start.43 = (bf16[48,384]{1,0:T(8,128)(2,1)S(1)}, bf16[48,384]{1,0:T(8,128)(2,1)S(1)}, u32[]{:S(2)}, u32[]{:S(2)}) collective-permute-start(bf16[48,384]{1,0:T(8,128)(2,1)S(1)} %fusion.127), channel_id=1, source_target_pairs={{0,16},{2,18},{4,20},{6,22},{8,24},{10,26},{12,28},{14,30},{16,0},... | collective-permute-start | bytes 110600 | tf_op jit(solution)/shard_map/ppermute | solution.py:19
  367.7 6.5 %collective-permute-start.33 = (bf16[48,384]{1,0:T(8,128)(2,1)S(1)}, bf16[48,384]{1,0:T(8,128)(2,1)S(1)}, u32[]{:S(2)}, u32[]{:S(2)}) collective-permute-start(bf16[48,384]{1,0:T(8,128)(2,1)S(1)} %fusion.128), channel_id=1, source_target_pairs={{0,16},{2,18},{4,20},{6,22},{8,24},{10,26},{12,28},{14,30},{16,0},... | collective-permute-start | bytes 110600 | tf_op jit(solution)/shard_map/ppermute | solution.py:19
  381.2 6.7 %collective-permute-start.45 = (bf16[192,384]{1,0:T(8,128)(2,1)S(1)}, bf16[192,384]{1,0:T(8,128)(2,1)S(1)}, u32[]{:S(2)}, u32[]{:S(2)}) collective-permute-start(bf16[192,384]{1,0:T(8,128)(2,1)S(1)} %pad_maximum_fusion.45), channel_id=1, source_target_pairs={{0,4},{2,6},{4,0},{6,2},{8,12},{10,14},{12,8},{14,10},{16,20},{18,... | collective-permute-start | bytes 442376 | tf_op jit(solution)/shard_map/ppermute | solution.py:19
  382.4 7.8 %collective-permute-start.35 = (bf16[192,384]{1,0:T(8,128)(2,1)S(1)}, bf16[192,384]{1,0:T(8,128)(2,1)S(1)}, u32[]{:S(2)}, u32[]{:S(2)}) collective-permute-start(bf16[192,384]{1,0:T(8,128)(2,1)S(1)} %pad_maximum_fusion.44), channel_id=1, source_target_pairs={{0,4},{2,6},{4,0},{6,2},{8,12},{10,14},{12,8},{14,10},{16,20},{18,... | collective-permute-start | bytes 442376 | tf_op jit(solution)/shard_map/ppermute | solution.py:19
  384.0 7.8 %collective-permute-start.25 = (bf16[192,384]{1,0:T(8,128)(2,1)S(1)}, bf16[192,384]{1,0:T(8,128)(2,1)S(1)}, u32[]{:S(2)}, u32[]{:S(2)}) collective-permute-start(bf16[192,384]{1,0:T(8,128)(2,1)S(1)} %pad_maximum_fusion.43), channel_id=1, source_target_pairs={{0,4},{2,6},{4,0},{6,2},{8,12},{10,14},{12,8},{14,10},{16,20},{18,... | collective-permute-start | bytes 442376 | tf_op jit(solution)/shard_map/ppermute | solution.py:19
  390.2 8.0 %collective-permute-start.46 = (bf16[384,384]{1,0:T(8,128)(2,1)S(1)}, bf16[384,384]{1,0:T(8,128)(2,1)S(1)}, u32[]{:S(2)}, u32[]{:S(2)}) collective-permute-start(bf16[384,384]{1,0:T(8,128)(2,1)S(1)} %pad_maximum_fusion.35), channel_id=1, source_target_pairs={{0,2},{2,0},{4,6},{6,4},{8,10},{10,8},{12,14},{14,12},{16,18},{18,... | collective-permute-start | bytes 884744 | tf_op jit(solution)/shard_map/ppermute | solution.py:19
  391.8 61.6 %collective-permute-start.36 = (bf16[384,384]{1,0:T(8,128)(2,1)}, bf16[384,384]{1,0:T(8,128)(2,1)}, u32[]{:S(2)}, u32[]{:S(2)}) collective-permute-start(bf16[384,384]{1,0:T(8,128)(2,1)} %pad_maximum_fusion.34), channel_id=1, source_target_pairs={{0,2},{2,0},{4,6},{6,4},{8,10},{10,8},{12,14},{14,12},{16,18},{18,... | collective-permute-start | bytes 884744 | tf_op jit(solution)/shard_map/ppermute | solution.py:19
  393.4 71.0 %collective-permute-start.26 = (bf16[384,384]{1,0:T(8,128)(2,1)}, bf16[384,384]{1,0:T(8,128)(2,1)}, u32[]{:S(2)}, u32[]{:S(2)}) collective-permute-start(bf16[384,384]{1,0:T(8,128)(2,1)} %pad_maximum_fusion.33), channel_id=1, source_target_pairs={{0,2},{2,0},{4,6},{6,4},{8,10},{10,8},{12,14},{14,12},{16,18},{18,... | collective-permute-start | bytes 884744 | tf_op jit(solution)/shard_map/ppermute | solution.py:19
  394.2 66.8 %collective-permute-start.61 = (bf16[192,768]{1,0:T(8,128)(2,1)}, bf16[192,768]{1,0:T(8,128)(2,1)}, u32[]{:S(2)}, u32[]{:S(2)}) collective-permute-start(bf16[192,768]{1,0:T(8,128)(2,1)} %pad_maximum_fusion.36), channel_id=1, source_target_pairs={{0,2},{2,0},{4,6},{6,4},{8,10},{10,8},{12,14},{14,12},{16,18},{18,... | collective-permute-start | bytes 884744 | tf_op jit(solution)/shard_map/ppermute | solution.py:19
  406.9 9.9 %collective-permute-start.68 = (bf16[384,384]{1,0:T(8,128)(2,1)S(1)}, bf16[384,384]{1,0:T(8,128)(2,1)S(1)}, u32[]{:S(2)}, u32[]{:S(2)}) collective-permute-start(bf16[384,384]{1,0:T(8,128)(2,1)S(1)} %fusion.101), channel_id=1, source_target_pairs={{0,8},{2,10},{4,12},{6,14},{8,0},{10,2},{12,4},{14,6},{16,24},{18,... | collective-permute-start | bytes 884744 | tf_op jit(solution)/shard_map/ppermute | solution.py:19
  410.9 14.6 %collective-permute-start.74 = (bf16[192,768]{1,0:T(8,128)(2,1)S(1)}, bf16[192,768]{1,0:T(8,128)(2,1)S(1)}, u32[]{:S(2)}, u32[]{:S(2)}) collective-permute-start(bf16[192,768]{1,0:T(8,128)(2,1)S(1)} %fusion.102), channel_id=1, source_target_pairs={{0,8},{2,10},{4,12},{6,14},{8,0},{10,2},{12,4},{14,6},{16,24},{18,... | collective-permute-start | bytes 884744 | tf_op jit(solution)/shard_map/ppermute | solution.py:19
  416.9 9.3 %collective-permute-start.69 = (bf16[192,384]{1,0:T(8,128)(2,1)S(1)}, bf16[192,384]{1,0:T(8,128)(2,1)S(1)}, u32[]{:S(2)}, u32[]{:S(2)}) collective-permute-start(bf16[192,384]{1,0:T(8,128)(2,1)S(1)} %fusion.118), channel_id=1, source_target_pairs={{0,16},{2,18},{4,20},{6,22},{8,24},{10,26},{12,28},{14,30},{16,0},... | collective-permute-start | bytes 442376 | tf_op jit(solution)/shard_map/ppermute | solution.py:19
  425.6 11.7 %collective-permute-start.75 = (bf16[96,768]{1,0:T(8,128)(2,1)S(1)}, bf16[96,768]{1,0:T(8,128)(2,1)S(1)}, u32[]{:S(2)}, u32[]{:S(2)}) collective-permute-start(bf16[96,768]{1,0:T(8,128)(2,1)S(1)} %fusion.119), channel_id=1, source_target_pairs={{0,16},{2,18},{4,20},{6,22},{8,24},{10,26},{12,28},{14,30},{16,0},... | collective-permute-start | bytes 442376 | tf_op jit(solution)/shard_map/ppermute | solution.py:19
  426.2 14.2 %collective-permute-start.70 = (bf16[192,384]{1,0:T(8,128)(2,1)S(1)}, bf16[192,384]{1,0:T(8,128)(2,1)S(1)}, u32[]{:S(2)}, u32[]{:S(2)}) collective-permute-start(bf16[192,384]{1,0:T(8,128)(2,1)S(1)} %fusion.104), channel_id=1, source_target_pairs={{0,16},{2,18},{4,20},{6,22},{8,24},{10,26},{12,28},{14,30},{16,0},... | collective-permute-start | bytes 442376 | tf_op jit(solution)/shard_map/ppermute | solution.py:19
  437.3 9.5 %collective-permute-start.76 = (bf16[96,768]{1,0:T(8,128)(2,1)S(1)}, bf16[96,768]{1,0:T(8,128)(2,1)S(1)}, u32[]{:S(2)}, u32[]{:S(2)}) collective-permute-start(bf16[96,768]{1,0:T(8,128)(2,1)S(1)} %fusion.103), channel_id=1, source_target_pairs={{0,16},{2,18},{4,20},{6,22},{8,24},{10,26},{12,28},{14,30},{16,0},... | collective-permute-start | bytes 442376 | tf_op jit(solution)/shard_map/ppermute | solution.py:19
  440.5 12.7 %collective-permute-start.71 = (bf16[384,384]{1,0:T(8,128)(2,1)S(1)}, bf16[384,384]{1,0:T(8,128)(2,1)S(1)}, u32[]{:S(2)}, u32[]{:S(2)}) collective-permute-start(bf16[384,384]{1,0:T(8,128)(2,1)S(1)} %pad_maximum_fusion.37), channel_id=1, source_target_pairs={{0,8},{2,10},{4,12},{6,14},{8,0},{10,2},{12,4},{14,6},{16,24},{18,... | collective-permute-start | bytes 884744 | tf_op jit(solution)/shard_map/ppermute | solution.py:19
  446.9 12.1 %collective-permute-start.77 = (bf16[192,768]{1,0:T(8,128)(2,1)S(1)}, bf16[192,768]{1,0:T(8,128)(2,1)S(1)}, u32[]{:S(2)}, u32[]{:S(2)}) collective-permute-start(bf16[192,768]{1,0:T(8,128)(2,1)S(1)} %pad_maximum_fusion.38), channel_id=1, source_target_pairs={{0,8},{2,10},{4,12},{6,14},{8,0},{10,2},{12,4},{14,6},{16,24},{18,... | collective-permute-start | bytes 884744 | tf_op jit(solution)/shard_map/ppermute | solution.py:19
  453.3 6.0 %collective-permute-start.72 = (bf16[768,384]{1,0:T(8,128)(2,1)S(1)}, bf16[768,384]{1,0:T(8,128)(2,1)S(1)}, u32[]{:S(2)}, u32[]{:S(2)}) collective-permute-start(bf16[768,384]{1,0:T(8,128)(2,1)S(1)} %pad_maximum_fusion.22), channel_id=1, source_target_pairs={{0,2},{2,0},{4,6},{6,4},{8,10},{10,8},{12,14},{14,12},{16,18},{18,... | collective-permute-start | bytes 1769480 | tf_op jit(solution)/shard_map/ppermute | solution.py:19
  459.7 28.8 %collective-permute-start.73 = (bf16[768,768]{1,0:T(8,128)(2,1)S(1)}, bf16[768,768]{1,0:T(8,128)(2,1)S(1)}, u32[]{:S(2)}, u32[]{:S(2)}) collective-permute-start(bf16[768,768]{1,0:T(8,128)(2,1)S(1)} %pad_maximum_fusion.6), channel_id=1, source_target_pairs={{0,4},{2,6},{4,0},{6,2},{8,12},{10,14},{12,8},{14,10},{16,20},{18,... | collective-permute-start | bytes 3538952 | tf_op jit(solution)/shard_map/ppermute | solution.py:19
  462.4 51.1 %collective-permute-start.79 = (bf16[768,768]{1,0:T(8,128)(2,1)S(1)}, bf16[768,768]{1,0:T(8,128)(2,1)S(1)}, u32[]{:S(2)}, u32[]{:S(2)}) collective-permute-start(bf16[768,768]{1,0:T(8,128)(2,1)S(1)} %pad_maximum_fusion.7), channel_id=1, source_target_pairs={{0,4},{2,6},{4,0},{6,2},{8,12},{10,14},{12,8},{14,10},{16,20},{18,... | collective-permute-start | bytes 3538952 | tf_op jit(solution)/shard_map/ppermute | solution.py:19
  (138 other events, 881.6 us)
